TPU v7x, 256 devices: a whole 4x4x8 slice. The times are simulated.
256 devices in a mesh: dp: 128 (over z, y, x_hi, core), rep: 2 (over x_lo).
Axes of the slice: x: 4 (x_hi: 2, x_lo: 2; x = x_hi * 2 + x_lo), y: 4, z: 8, core: 2. Of those that a mesh axis runs over, the one named last changes fastest.
Arguments:
- images: bfloat16 [2, 32768, 1152], P('rep', 'dp'), may hold values from -6 to 6
- texts: bfloat16 [2, 32768, 1152], P('rep', 'dp'), may hold values from -6 to 6
- img_head: bfloat16 [1152, 1152], replicated, may hold values from -0.1875 to 0.1875
- txt_head: bfloat16 [1152, 1152], replicated, may hold values from -0.1875 to 0.1875
- log_scale: float32 [], replicated, may hold values from 3 to 3.6
- bias: float32 [], replicated, may hold values from -3 to -1
Outputs:
- row_losses: float32 [2, 32768], P('rep', 'dp')
- head_grads: float32 [2304, 1152], P(('dp', 'rep'))
All inputs are finite; a program needn't handle non-finite values.
Results may differ from a plain program's by a relative error of at most 0.0025.
Values may be sent and summed in bfloat16 or wider, within the bound.
No kernel may reach another device: no remote copies, remote signals or barrier semaphores. Data moves between devices by JAX's collectives and lax.ppermute only.
A program may use at most 128 MiB of HBM per device.

v0:
```python
import jax
import jax.numpy as jnp
from jax import lax
from jax.sharding import PartitionSpec as P

STEPS = 4


def passed_along(array, axis, by):
    devices = lax.axis_size(axis)
    return lax.ppermute(array, axis, [(i, (i + by) % devices) for i in range(devices)])


def normed(feats, head):
    u = jnp.dot(feats, head, preferred_element_type=jnp.float32)
    inv = lax.rsqrt(jnp.sum(u * u, axis=-1, keepdims=True) + 1e-06)
    return (u * inv, inv)


def backnorm(grad, zfull, inv):
    return (inv * (grad - zfull * jnp.sum(grad * zfull, axis=-1, keepdims=True))).astype(
        jnp.bfloat16
    )


def tile_grad(query, key_block, labels, scale, bias, block):
    logits = scale * jnp.dot(query, key_block.T, preferred_element_type=jnp.float32) + bias
    gt_tile = (scale * (-labels * jax.nn.sigmoid(-labels * logits)) / block).astype(jnp.bfloat16)
    return (logits, gt_tile)


def score_tile(query, key_block, labels, scale, bias, block):
    logits, gt_tile = tile_grad(query, key_block, labels, scale, bias, block)
    loss_row = jnp.sum(jax.nn.softplus(-labels * logits), axis=1)
    dq = jnp.dot(gt_tile, key_block, preferred_element_type=jnp.float32)
    dk = jnp.dot(gt_tile.T, query, preferred_element_type=jnp.float32)
    return (loss_row, dq, dk)


def local(images, texts, img_head, txt_head, log_scale, bias):
    f_img = images[0]
    f_txt = texts[0]
    block = f_img.shape[0]
    width = f_img.shape[1]
    scale = jnp.exp(log_scale)
    ident = jnp.eye(block, dtype=jnp.float32)
    zf_img, inv_img = normed(f_img, img_head)
    zf_txt, inv_txt = normed(f_txt, txt_head)
    z_img = zf_img.astype(jnp.bfloat16)
    z_txt = zf_txt.astype(jnp.bfloat16)
    row_loss = jnp.zeros((block,), jnp.float32)
    g_img = jnp.zeros((block, width), jnp.float32)
    current = z_txt
    buffer = jnp.zeros((block, width), jnp.float32)
    for step in range(STEPS):
        if step > 0:
            current = passed_along(current, "dp", 1)
            buffer = passed_along(buffer, "dp", 1)
        labels = 2.0 * ident - 1.0 if step == 0 else -jnp.ones_like(ident)
        loss_row, dq, dk = score_tile(z_img, current, labels, scale, bias, block)
        row_loss = row_loss + loss_row
        g_img = g_img + dq
        buffer = buffer + dk
    g_txt = passed_along(buffer, "dp", 1 - STEPS)
    du_img = backnorm(g_img, zf_img, inv_img)
    du_txt = backnorm(g_txt, zf_txt, inv_txt)
    term = jnp.concatenate(
        [
            jnp.dot(f_img.T, du_img, preferred_element_type=jnp.float32),
            jnp.dot(f_txt.T, du_txt, preferred_element_type=jnp.float32),
        ],
        axis=0,
    )
    shares = lax.psum_scatter(term, ("dp", "rep"), scatter_dimension=0, tiled=True)
    return (row_loss[None, :], shares)


def solution(mesh):
    placed = (P("rep", "dp", None), P("rep", "dp", None), P(), P(), P(), P())
    return jax.shard_map(
        local,
        mesh=mesh,
        in_specs=placed,
        out_specs=(P("rep", "dp"), P(("dp", "rep"), None)),
        check_vma=False,
    )
```

profile of v0, /device:TPU:1, one launch (start us, length us, event | category | flops | bytes accessed | tf_op | source)
XLA Modules:
  0.0 430.9 jit_solution(22329454713191726)
XLA Ops:
  8.0 0.9 copy-done
  8.9 3.2 multiply_reduce_fusion.3
  12.2 2.1 multiply_reduce_fusion.2
  15.0 1.5 multiply_convert_fusion.3
  16.7 0.5 fusion.15
  17.6 4.2 collective-permute-start.3
  21.9 19.4 %collective-permute-done = bf16[256,1152]{1,0:T(8,128)(2,1)S(1)} collective-permute-done((bf16[256,1152]{1,0:T(8,128)(2,1)S(1)}, bf16[256,1152]{1,0:T(8,128)(2,1)S(1)}, u32[]{:S(2)}, u32[]{:S(2)}) %collective-permute-start) | collective-permute-done | bytes 589856 | tf_op jit(solution)/shard_map/ppermute | solution.py:11
  41.3 0.5 fusion.16
  42.2 4.1 collective-permute-start.4
  46.3 19.4 %collective-permute-done.1 = bf16[256,1152]{1,0:T(8,128)(2,1)S(1)} collective-permute-done((bf16[256,1152]{1,0:T(8,128)(2,1)S(1)}, bf16[256,1152]{1,0:T(8,128)(2,1)S(1)}, u32[]{:S(2)}, u32[]{:S(2)}) %collective-permute-start.1) | collective-permute-done | bytes 589856 | tf_op jit(solution)/shard_map/ppermute | solution.py:11
  66.8 4.1 collective-permute-start.5
  71.3 19.0 %collective-permute-done.2 = bf16[256,1152]{1,0:T(8,128)(2,1)S(1)} collective-permute-done((bf16[256,1152]{1,0:T(8,128)(2,1)S(1)}, bf16[256,1152]{1,0:T(8,128)(2,1)S(1)}, u32[]{:S(2)}, u32[]{:S(2)}) %collective-permute-start.2) | collective-permute-done | bytes 589856 | tf_op jit(solution)/shard_map/ppermute | solution.py:11
  90.3 0.5 fusion.18
  91.3 12.0 %collective-permute-start.6 = (f32[256,1152]{1,0:T(8,128)S(1)}, f32[256,1152]{1,0:T(8,128)S(1)}, u32[]{:S(2)}, u32[]{:S(2)}) collective-permute-start(f32[256,1152]{1,0:T(8,128)S(1)} %add.139), channel_id=1, source_target_pairs={{0,250},{2,252},{4,254},{6,0},{8,2},{10,4},{12,6},{14,8},{16,10},{... | collective-permute-start | bytes 3538952 | tf_op jit(solution)/shard_map/ppermute | solution.py:11
  104.2 0.8 copy-done.2
  105.0 0.5 multiply_reduce_fusion.1
  105.5 0.5 copy-done.3
  106.1 3.4 convolution_bitcast_fusion.1
  109.5 14.2 %collective-permute-done.6 = f32[256,1152]{1,0:T(8,128)S(1)} collective-permute-done((f32[256,1152]{1,0:T(8,128)S(1)}, f32[256,1152]{1,0:T(8,128)S(1)}, u32[]{:S(2)}, u32[]{:S(2)}) %collective-permute-start.6) | collective-permute-done | bytes 1179680 | tf_op jit(solution)/shard_map/ppermute | solution.py:11
  124.0 3.5 convolution_bitcast_fusion
  127.5 8.8 %pad_maximum_fusion = f32[2304,1152]{1,0:T(8,128)} fusion(f32[1152,1152]{1,0:T(8,128)} %convolution_bitcast_fusion, f32[1152,1152]{1,0:T(8,128)} %convolution_bitcast_fusion.1), kind=kLoop, calls=%fused_computation | loop fusion | flops 2654208 | bytes 21233664 | tf_op jit(solution)/shard_map/concatenate | solution.py:67
  136.4 0.6 add_add_fusion
  136.9 285.6 %all-reduce.3.cloned.1.call-done = f32[2304,1152]{1,0:T(8,128)} async-done(((f32[2304,1152]{1,0:T(8,128)}), f32[2304,1152]{1,0:T(8,128)}) %all-reduce.3.cloned.1.call-update) | async-done | bytes 10616848
  422.5 1.5 constant_dynamic-slice_fusion
  (31 shorter events, 4.4 us)
Async XLA Ops:
  7.2 1.8 copy-start
  7.2 415.3 %all-reduce.3.cloned.1.call-start = ((), (), s32[]{:S(2)}) async-start(), calls=%async_computation | async-start | bytes 21233664
  8.9 3.2 copy-start.4
  8.9 3.2 copy-start.5
  14.9 1.6 copy-start.1
  17.6 24.2 %collective-permute-start.3 = (f32[256,1152]{1,0:T(8,128)S(1)}, f32[256,1152]{1,0:T(8,128)S(1)}, u32[]{:S(2)}, u32[]{:S(2)}) collective-permute-start(f32[256,1152]{1,0:T(8,128)S(1)} %fusion.21), channel_id=1, source_target_pairs={{0,2},{2,4},{4,6},{6,8},{8,10},{10,12},{12,14},{14,16},{16,18},{18... | collective-permute-start | bytes 3538952 | tf_op jit(solution)/shard_map/ppermute | solution.py:11
  21.8 19.5 %collective-permute-start = (bf16[256,1152]{1,0:T(8,128)(2,1)S(1)}, bf16[256,1152]{1,0:T(8,128)(2,1)S(1)}, u32[]{:S(2)}, u32[]{:S(2)}) collective-permute-start(bf16[256,1152]{1,0:T(8,128)(2,1)S(1)} %multiply_convert_fusion.2), channel_id=1, source_target_pairs={{0,2},{2,4},{4,6},{6,8},{8,10},{10,12},{12,14},{14,16},{16,18},{18... | collective-permute-start | bytes 1769480 | tf_op jit(solution)/shard_map/ppermute | solution.py:11
  42.2 24.4 %collective-permute-start.4 = (f32[256,1152]{1,0:T(8,128)S(1)}, f32[256,1152]{1,0:T(8,128)S(1)}, u32[]{:S(2)}, u32[]{:S(2)}) collective-permute-start(f32[256,1152]{1,0:T(8,128)S(1)} %convolution_add_fusion), channel_id=1, source_target_pairs={{0,2},{2,4},{4,6},{6,8},{8,10},{10,12},{12,14},{14,16},{16,18},{18... | collective-permute-start | bytes 3538952 | tf_op jit(solution)/shard_map/ppermute | solution.py:11
  46.2 19.5 %collective-permute-start.1 = (bf16[256,1152]{1,0:T(8,128)(2,1)S(1)}, bf16[256,1152]{1,0:T(8,128)(2,1)S(1)}, u32[]{:S(2)}, u32[]{:S(2)}) collective-permute-start(bf16[256,1152]{1,0:T(8,128)(2,1)S(1)} %collective-permute-done), channel_id=1, source_target_pairs={{0,2},{2,4},{4,6},{6,8},{8,10},{10,12},{12,14},{14,16},{16,18},{18... | collective-permute-start | bytes 1769480 | tf_op jit(solution)/shard_map/ppermute | solution.py:11
  66.8 24.4 %collective-permute-start.5 = (f32[256,1152]{1,0:T(8,128)S(1)}, f32[256,1152]{1,0:T(8,128)S(1)}, u32[]{:S(2)}, u32[]{:S(2)}) collective-permute-start(f32[256,1152]{1,0:T(8,128)S(1)} %add.138), channel_id=1, source_target_pairs={{0,2},{2,4},{4,6},{6,8},{8,10},{10,12},{12,14},{14,16},{16,18},{18... | collective-permute-start | bytes 3538952 | tf_op jit(solution)/shard_map/ppermute | solution.py:11
  70.8 19.5 %collective-permute-start.2 = (bf16[256,1152]{1,0:T(8,128)(2,1)S(1)}, bf16[256,1152]{1,0:T(8,128)(2,1)S(1)}, u32[]{:S(2)}, u32[]{:S(2)}) collective-permute-start(bf16[256,1152]{1,0:T(8,128)(2,1)S(1)} %collective-permute-done.1), channel_id=1, source_target_pairs={{0,2},{2,4},{4,6},{6,8},{8,10},{10,12},{12,14},{14,16},{16,18},{18... | collective-permute-start | bytes 1769480 | tf_op jit(solution)/shard_map/ppermute | solution.py:11
  91.3 32.4 %collective-permute-start.6 = (f32[256,1152]{1,0:T(8,128)S(1)}, f32[256,1152]{1,0:T(8,128)S(1)}, u32[]{:S(2)}, u32[]{:S(2)}) collective-permute-start(f32[256,1152]{1,0:T(8,128)S(1)} %add.139), channel_id=1, source_target_pairs={{0,250},{2,252},{4,254},{6,0},{8,2},{10,4},{12,6},{14,8},{16,10},{... | collective-permute-start | bytes 3538952 | tf_op jit(solution)/shard_map/ppermute | solution.py:11
  103.7 1.3 copy-start.2
  105.0 1.1 copy-start.3
Sparse Core Ops, SparseCore 0:
  136.5 285.9 all-reduce.2
where the time goes:
time: 432 us; the launch traced here: 431 us
  waiting for transfers between devices  358 us (83%)
  starting transfers between devices  24.6 us (6%)
  matrix products  17.5 us (4%)
  between operations  15.6 us (4%)
  other arithmetic  11.6 us (3%)
    unnamed x2, waiting for transfers between devices  286 us
    ppermute x7, waiting for transfers between devices, passed_along(): lax.ppermute(array, axis, [(i, (i + by) % devices) for i in range(devices)])  72 us
    ppermute x7, starting transfers between devices, passed_along(): lax.ppermute(array, axis, [(i, (i + by) % devices) for i in range(devices)])  24.6 us
    concatenate x1, other arithmetic, local(): jnp.concatenate([jnp.dot(f_img.T, du_img, preferred_element_type=jnp.floa...  8.78 us
  transfers between devices with their start and end apart: 8, of which 5 were waited for; matrix products, arithmetic and copies ran while one was open for 2% of the time, Pallas kernels for 0%

commit v1 on v0

v1 whole, which is shorter than its diff:
```python
import jax
import jax.numpy as jnp
import numpy as np
from jax import lax
from jax.sharding import Mesh, PartitionSpec as P

AXES = ("z", "y", "xh", "c", "xl")
NZ, NY, NX = 8, 4, 4
BLOCK = 256
ROWS9 = 9


def place(i):
    return i // 32, (i // 8) % 4, ((i // 4) % 2) * 2 + i % 2, (i // 2) % 2


def index(z, y, x, c):
    return (((z * NY + y) * 2 + x // 2) * 2 + c) * 2 + x % 2


def chip_shift(by):
    pairs = []
    for i in range(256):
        z, y, x, c = place(i)
        q = (((z * NY + y) * 2 + x // 2) + by) % 64
        pairs.append((i, index(q // 8, (q // 2) % 4, (q % 2) * 2 + x % 2, c)))
    return pairs


def core_swap():
    return [(i, index(*place(i)[:3], 1 - place(i)[3])) for i in range(256)]


def grouped(key, order):
    found = {}
    for i in range(256):
        found.setdefault(key(*place(i)), []).append(i)
    return [sorted(v, key=lambda i: order(*place(i))) for v in found.values()]


def first_groups():
    return grouped(
        lambda z, y, x, c: (c, y, z // 2) if c == 0 else (c, x, ((z + 1) % NZ) // 2),
        lambda z, y, x, c: (z % 2, x if c == 0 else y),
    )


def second_groups():
    return grouped(
        lambda z, y, x, c: (c, x if c == 0 else y, z % 2),
        lambda z, y, x, c: (z // 2, y if c == 0 else x),
    )


def row_order():
    out = np.zeros((2, 2, 576), np.int32)
    for c in range(2):
        for modality in range(2):
            rows = []
            for zl in range(2):
                for a in range(4):
                    for zh in (2 * modality, 2 * modality + 1):
                        for b in range(4):
                            x, y = (a, b) if c == 0 else (b, a)
                            first = 9 * index(2 * zh + zl, y, x, c) - 1152 * modality
                            rows.extend(range(first, first + 9))
            out[c, modality] = rows
    return out


def normed(feats, head):
    u = jnp.dot(feats, head, preferred_element_type=jnp.float32)
    inv = lax.rsqrt(jnp.sum(u * u, axis=-1, keepdims=True) + 1e-06)
    return (u * inv, inv)


def backnorm(grad, zfull, inv):
    return (inv * (grad - zfull * jnp.sum(grad * zfull, axis=-1, keepdims=True))).astype(
        jnp.bfloat16
    )


def local(images, texts, img_head, txt_head, log_scale, bias):
    img, txt = images[0], texts[0]
    c = lax.axis_index("c")
    first = c == 0
    scale = jnp.exp(log_scale)

    def swap(a):
        return lax.ppermute(a, AXES, core_swap())

    near = lax.ppermute(txt, AXES, chip_shift(1))
    other_img, other_txt = swap(img), swap(txt)
    far = lax.ppermute(jnp.where(first, other_txt[:128], txt[128:]), AXES, chip_shift(2))
    passed = swap(jnp.concatenate([near, far], axis=0))
    near_o, far_o = passed[:256], passed[256:]
    f_txt = jnp.where(
        first,
        jnp.concatenate([far, far_o, near, near_o, txt, other_txt], axis=0),
        jnp.concatenate([far_o, far, near_o, near, other_txt, txt], axis=0),
    )
    f_img = jnp.where(
        first, jnp.concatenate([img, other_img], 0), jnp.concatenate([other_img, img], 0)
    )
    zf_img, inv_img = normed(f_img, img_head)
    zf_txt, inv_txt = normed(f_txt, txt_head)
    z_img = zf_img.astype(jnp.bfloat16)
    z_txt = zf_txt.astype(jnp.bfloat16)

    col = lax.broadcasted_iota(jnp.int32, (BLOCK, 4 * BLOCK), 1)
    row = lax.broadcasted_iota(jnp.int32, (BLOCK, 4 * BLOCK), 0)
    labels = jnp.where(col == row + 3 * BLOCK, 1.0, -1.0)
    losses, g_img, g_txt = [], [], jnp.zeros((5 * BLOCK, 1152), jnp.float32)
    for d in range(2):
        q = z_img[d * BLOCK : (d + 1) * BLOCK]
        k = z_txt[d * BLOCK : (d + 4) * BLOCK]
        logits = scale * jnp.dot(q, k.T, preferred_element_type=jnp.float32) + bias
        gt = (scale * (-labels * jax.nn.sigmoid(-labels * logits)) / BLOCK).astype(jnp.bfloat16)
        losses.append(jnp.sum(jax.nn.softplus(-labels * logits), axis=1))
        g_img.append(jnp.dot(gt, k, preferred_element_type=jnp.float32))
        dk = jnp.dot(gt.T, q, preferred_element_type=jnp.float32)
        g_txt = g_txt.at[d * BLOCK : (d + 4) * BLOCK].add(dk)
    loss = jnp.where(first, losses[0], losses[1])
    du_img = backnorm(jnp.concatenate(g_img, 0), zf_img, inv_img)
    du_txt = backnorm(g_txt, zf_txt, inv_txt)

    order = jnp.asarray(row_order())[c]
    pick = (lax.broadcasted_iota(jnp.int32, (2, 576, 1152), 2) == order[:, :, None]).astype(jnp.bfloat16)
    terms = []
    for f, du, p in ((f_img, du_img, pick[0]), (f_txt, du_txt, pick[1])):
        ft = jnp.dot(p, f.T, preferred_element_type=jnp.float32).astype(jnp.bfloat16)
        terms.append(jnp.dot(ft, du, preferred_element_type=jnp.float32).reshape(8, 72, 1152))
    term = jnp.concatenate(terms, axis=1).astype(jnp.bfloat16)
    got = lax.all_to_all(term.reshape(1152, 1152), AXES, 0, 0, axis_index_groups=first_groups(), tiled=True)
    half = jnp.sum(got.reshape(8, 16, 9, 1152).astype(jnp.float32), axis=0)
    half = half.reshape(16, 81, 128).astype(jnp.bfloat16)
    half = jnp.pad(half, ((0, 0), (0, 7), (0, 0))).reshape(16 * 88, 128)
    got = lax.all_to_all(half, AXES, 0, 0, axis_index_groups=second_groups(), tiled=True)
    shares = jnp.sum(got.reshape(16, 88, 128).astype(jnp.float32), axis=0)[:81].reshape(9, 1152)
    return (loss[None, :], shares)


def solution(mesh):
    inner = Mesh(mesh.devices.reshape(NZ, NY, 2, 2, 2), AXES)
    dp = ("z", "y", "xh", "c")
    placed = (P("xl", dp, None), P("xl", dp, None), P(), P(), P(), P())
    return jax.shard_map(
        local,
        mesh=inner,
        in_specs=placed,
        out_specs=(P("xl", dp), P(AXES, None)),
        check_vma=False,
    )
```

time: 432 us -> 122 us (0.28)
  waiting for transfers between devices: 358 us -> 29.2 us
  blocking collectives: 0 us -> 23.5 us
  matrix products: 17.5 us -> 33.8 us
  between operations: 15.6 us -> 2.27 us
  starting transfers between devices: 24.6 us -> 15.5 us
    unnamed x2 -> x0, waiting for transfers between devices: 286 us -> none
    ppermute x7 -> x5, waiting for transfers between devices: 72 us -> 17.3 us  [the longest x1 13.7 us: local(): near = lax.ppermute(txt, AXES, chip_shift(1))]
    all_to_all x0 -> x1, blocking collectives: none -> 23.5 us  [local(): lax.all_to_all(term.reshape(1152, 1152), AXES, 0, 0, axis_index_groups=fi...]
    ppermute x7 -> x5, starting transfers between devices: 24.6 us -> 7.59 us  [the longest x1 3.65 us: local(): near = lax.ppermute(txt, AXES, chip_shift(1))]
    dot_general x14 -> x8, matrix products: 12.2 us -> 25.2 us  [the longest x2 17.2 us: local(): jnp.dot(ft, du, preferred_element_type=jnp.float32).reshape(8, 72, 1152)]
    all_to_all x0 -> x1, waiting for transfers between devices: none -> 12 us  [local(): lax.all_to_all(half, AXES, 0, 0, axis_index_groups=second_groups(), tiled...]
    all_to_all x0 -> x1, starting transfers between devices: none -> 7.91 us  [local(): lax.all_to_all(half, AXES, 0, 0, axis_index_groups=second_groups(), tiled...]
    concatenate x1 -> x2, other arithmetic: 8.78 us -> 1.99 us  [the longest x1 1.92 us: local(): term = jnp.concatenate(terms, axis=1).astype(jnp.bfloat16)]
  transfers between devices with their start and end apart: 8 -> 6, of which waited for: 5 -> 4; matrix products, arithmetic and copies ran while one was open for 2% -> 7% of each run, Pallas kernels for 0% -> 0%
where the time goes in v1:
time: 122 us
  matrix products  33.8 us (28%)
  waiting for transfers between devices  29.2 us (24%)
  blocking collectives  23.5 us (19%)
  starting transfers between devices  15.5 us (13%)
  other arithmetic  9.67 us (8%)
  local copies, waits for them, and re-layouts  7.94 us (7%)
  between operations  2.27 us (2%)
    all_to_all x1, blocking collectives, local(): lax.all_to_all(term.reshape(1152, 1152), AXES, 0, 0, axis_index_groups=fi...  23.5 us
    dot_general x2, matrix products, local(): jnp.dot(ft, du, preferred_element_type=jnp.float32).reshape(8, 72, 1152)  17.2 us
    ppermute x1, waiting for transfers between devices, local(): near = lax.ppermute(txt, AXES, chip_shift(1))  13.7 us
    all_to_all x1, waiting for transfers between devices, local(): lax.all_to_all(half, AXES, 0, 0, axis_index_groups=second_groups(), tiled...  12 us
    dot_general x2, matrix products, normed(): u = jnp.dot(feats, head, preferred_element_type=jnp.float32)  8.56 us
    all_to_all x1, starting transfers between devices, local(): lax.all_to_all(half, AXES, 0, 0, axis_index_groups=second_groups(), tiled...  7.91 us
    ppermute x1, starting transfers between devices, local(): near = lax.ppermute(txt, AXES, chip_shift(1))  3.65 us
    unnamed x25, local copies, waits for them, and re-layouts  3.27 us
  transfers between devices with their start and end apart: 6, of which 4 were waited for; matrix products, arithmetic and copies ran while one was open for 7% of the time, Pallas kernels for 0%

profile of v1, /device:TPU:1, one launch (start us, length us, event | category | flops | bytes accessed | tf_op | source)
XLA Modules:
  0.0 121.9 jit_solution(14485888799222684018)
XLA Ops:
  0.6 3.7 %collective-permute-start.3 = (bf16[256,1152]{1,0:T(8,128)(2,1)}, bf16[256,1152]{1,0:T(8,128)(2,1)S(1)}, u32[]{:S(2)}, u32[]{:S(2)}) collective-permute-start(bf16[256,1152]{1,0:T(8,128)(2,1)} %bitcast.26), channel_id=1, source_target_pairs={{0,4},{1,5},{2,6},{3,7},{4,8},{5,9},{6,10},{7,11},{8,12},{9,13},{1... | collective-permute-start | bytes 1769480 | tf_op jit(solution)/shard_map/ppermute | solution.py:92
  7.3 1.9 %iota_compare_fusion = pred[2,576,1152]{2,1,0:T(32,128)(4,1)} fusion(s32[2,576]{1,0:T(2,128)S(1)} %dynamic-slice_bitcast_fusion), kind=kLoop, calls=%fused_computation.3 | loop fusion | flops 1327104 | bytes 1331712 | tf_op jit(solution)/shard_map/eq | solution.py:128
  10.3 1.4 %collective-permute-start.2 = (bf16[128,1152]{1,0:T(8,128)(2,1)S(1)}, bf16[128,1152]{1,0:T(8,128)(2,1)S(1)}, u32[]{:S(2)}, u32[]{:S(2)}) collective-permute-start(bf16[128,1152]{1,0:T(8,128)(2,1)S(1)} %slice_select_fusion), channel_id=1, source_target_pairs={{0,8},{1,9},{2,10},{3,11},{4,12},{5,13},{6,14},{7,15},{8,16},{9,17... | collective-permute-start | bytes 884744 | tf_op jit(solution)/shard_map/ppermute | solution.py:94
  11.7 4.4 %multiply_reduce_fusion.3 = (f32[512]{0:T(512)S(1)}, f32[512,1152]{1,0:T(8,128)S(1)}) fusion(bf16[1152,1152]{1,0:T(8,128)(2,1)} %param.13, bf16[256,1152]{1,0:T(8,128)(2,1)} %collective-permute-done, bf16[256,1152]{1,0:T(8,128)(2,1)} %bitcast.33, pred[]{:T(512)S(6)} %eq.22), kind=kOutput, calls=%fused_computation.22 | convolution fusion | flops 1365442048 | bytes 6195201 | tf_op jit(solution)/shard_map/dot_general | solution.py:72
  16.1 13.7 %collective-permute-done.3 = bf16[256,1152]{1,0:T(8,128)(2,1)S(1)} collective-permute-done((bf16[256,1152]{1,0:T(8,128)(2,1)}, bf16[256,1152]{1,0:T(8,128)(2,1)S(1)}, u32[]{:S(2)}, u32[]{:S(2)}) %collective-permute-start.3) | collective-permute-done | bytes 589856 | tf_op jit(solution)/shard_map/ppermute | solution.py:92
  29.7 1.8 %collective-permute-done.2 = bf16[128,1152]{1,0:T(8,128)(2,1)S(1)} collective-permute-done((bf16[128,1152]{1,0:T(8,128)(2,1)S(1)}, bf16[128,1152]{1,0:T(8,128)(2,1)S(1)}, u32[]{:S(2)}, u32[]{:S(2)}) %collective-permute-start.2) | collective-permute-done | bytes 294944 | tf_op jit(solution)/shard_map/ppermute | solution.py:94
  31.6 1.6 %collective-permute-start.4 = (bf16[384,1152]{1,0:T(8,128)(2,1)S(1)}, bf16[384,1152]{1,0:T(8,128)(2,1)S(1)}, u32[]{:S(2)}, u32[]{:S(2)}) collective-permute-start(bf16[384,1152]{1,0:T(8,128)(2,1)S(1)} %pad_maximum_fusion.2), channel_id=1, source_target_pairs={{0,2},{1,3},{2,0},{3,1},{4,6},{5,7},{6,4},{7,5},{8,10},{9,11},{10,... | collective-permute-start | bytes 2654216 | tf_op jit(solution)/shard_map/ppermute | solution.py:90
  33.4 1.8 %collective-permute-done.4 = bf16[384,1152]{1,0:T(8,128)(2,1)S(1)} collective-permute-done((bf16[384,1152]{1,0:T(8,128)(2,1)S(1)}, bf16[384,1152]{1,0:T(8,128)(2,1)S(1)}, u32[]{:S(2)}, u32[]{:S(2)}) %collective-permute-start.4) | collective-permute-done | bytes 884768 | tf_op jit(solution)/shard_map/ppermute | solution.py:90
  35.7 1.1 constant_dynamic-update-slice_fusion.5
  37.0 1.6 %constant_dynamic-update-slice_fusion = bf16[1280,1152]{1,0:T(8,128)(2,1)S(1)} fusion(bf16[1280,1152]{1,0:T(8,128)(2,1)S(1)} %get-tuple-element.31, bf16[256,1152]{1,0:T(8,128)(2,1)} %collective-permute-done.1), kind=kLoop, calls=%fused_computation.62 | loop fusion | bytes 1179648 | tf_op jit(solution)/shard_map/concatenate | solution.py:99
  38.6 4.2 %multiply_reduce_fusion.1 = (f32[1280]{0:T(1024)S(1)}, f32[1280,1152]{0,1:T(8,128)S(1)}) fusion(bf16[1152,1152]{1,0:T(8,128)(2,1)S(1)} %copy-done, bf16[1280,1152]{1,0:T(8,128)(2,1)S(1)} %constant_dynamic-update-slice_fusion, bf16[1280,1152]{1,0:T(8,128)(2,1)S(1)} %get-tuple-element.30, pred[]{:T(512)S(6)} %eq.22), kind=kOutput, calls=%fused_computation.2 | convolution fusion | flops 3401808640 | bytes 14455809 | tf_op jit(solution)/shard_map/dot_general | solution.py:72
  43.3 1.5 %fusion.35 = (f32[256]{0:T(256)S(1)}, f32[256,1024]{1,0:T(8,128)S(1)}) fusion(f32[]{:T(128)S(6)} %copy.28, bf16[1280,1152]{0,1:T(8,128)(2,1)S(1)} %multiply_convert_fusion.1, bf16[512,1152]{1,0:T(8,128)(2,1)S(1)} %multiply_convert_fusion.4, f32[]{:T(128)S(6)} %exp.16, s32[256]{0:T(256)S(1)} %iota_add_fusion), kind=kOutput, calls=%fused_computation.44 | convolution fusion | flops 607387392 | bytes 3999752 | tf_op jit(solution)/shard_map/dot_general | solution.py:117
  44.7 1.4 %fusion.34 = (f32[256]{0:T(256)S(1)}, f32[256,1024]{1,0:T(8,128)S(1)}) fusion(f32[]{:T(128)S(6)} %copy.28, bf16[1280,1152]{0,1:T(8,128)(2,1)S(1)} %multiply_convert_fusion.1, bf16[512,1152]{1,0:T(8,128)(2,1)S(1)} %multiply_convert_fusion.4, f32[]{:T(128)S(6)} %exp.16, s32[256]{0:T(256)S(1)} %iota_add_fusion), kind=kOutput, calls=%fused_computation.43 | convolution fusion | flops 607387392 | bytes 3999752 | tf_op jit(solution)/shard_map/dot_general | solution.py:117
  46.2 1.1 fusion.8
  47.3 1.1 fusion.38
  50.1 1.8 %fusion = f32[1280,1152]{0,1:T(8,128)S(1)} fusion(f32[1280,1152]{0,1:T(8,128)S(1)} %scatter-add.6, bf16[512,1152]{1,0:T(8,128)(2,1)S(1)} %multiply_convert_fusion.4, f32[256,1024]{1,0:T(8,128)S(1)} %get-tuple-element.39, f32[]{:T(128)S(6)} %exp.16, s32[256]{0:T(256)S(1)} %iota_add_fusion), kind=kOutput, calls=%fused_computation.6 | convolution fusion | flops 607780864 | bytes 11076612 | tf_op jit(solution)/shard_map/dot_general | solution.py:121
  52.8 1.7 %copy-done.2 = f32[1280,1152]{0,1:T(8,128)} copy-done((f32[1280,1152]{0,1:T(8,128)}, f32[1280,1152]{0,1:T(8,128)S(1)}, u32[]{:S(2)}) %copy-start.2) | copy-done | bytes 5898264
  54.8 10.8 %convolution_convert_fusion = bf16[576,1152]{1,0:T(8,128)(2,1)} fusion(f32[1280,1152]{0,1:T(8,128)} %copy-done.2, f32[1280,1152]{0,1:T(8,128)} %copy-done.1, f32[1280]{0:T(1024)S(1)} %multiply_reduce_fusion, f32[1280]{0:T(1024)S(1)} %add_rsqrt_fusion, pred[2,576,1152]{2,1,0:T(32,128)(4,1)} %iota_compare_fusion, bf16[1280,1152]{1,0:T(8,128)(2,1)} %copy-done.8, ...), kind=kOutput, calls=%fused_computation.9 | convolution fusion | flops 3407634432 | bytes 19695616 | tf_op jit(solution)/shard_map/dot_general | solution.py:132
  65.6 6.3 %convolution_convert_fusion.2 = bf16[576,1152]{1,0:T(8,128)(2,1)} fusion(f32[512,1152]{1,0:T(8,128)} %copy-done.3, f32[256,1152]{1,0:T(8,128)} %copy-done.6, f32[256,1152]{1,0:T(8,128)} %copy-done.5, f32[512]{0:T(512)S(1)} %multiply_reduce_fusion.2, f32[512]{0:T(512)S(1)} %add_rsqrt_fusion.1, pred[2,576,1152]{2,1,0:T(32,128)(4,1)} %iota_compare_fusion, ...), kind=kOutput, calls=%fused_computation.11 | convolution fusion | flops 1368760320 | bytes 7892993 | tf_op jit(solution)/shard_map/dot_general | solution.py:132
  72.0 1.9 %pad_maximum_fusion = bf16[8,144,1152]{2,1,0:T(8,128)(2,1)S(1)} fusion(bf16[8,72,1152]{2,1,0:T(8,128)(2,1)} %bitcast.28, bf16[8,72,1152]{2,1,0:T(8,128)(2,1)} %bitcast.29), kind=kLoop, calls=%fused_computation.15 | loop fusion | flops 5308416 | bytes 5308416 | tf_op jit(solution)/shard_map/concatenate | solution.py:133
  73.9 23.5 %all_to_all.12 = bf16[8,144,1152]{2,1,0:T(8,128)(2,1)} all-to-all(bf16[8,144,1152]{2,1,0:T(8,128)(2,1)S(1)} %pad_maximum_fusion), channel_id=1, replica_groups={{0,1,4,5,32,33,36,37},{2,10,18,26,226,234,242,250},{3,11,19,27,227,235,..., dimensions={0} | all-to-all | bytes 5308416 | tf_op jit(solution)/shard_map/all_to_all | solution.py:134
  97.4 2.2 %reduce_sum.81 = bf16[144,1152]{1,0:T(8,128)(2,1)S(1)} reduce(bf16[8,144,1152]{2,1,0:T(8,128)(2,1)} %all_to_all.12, bf16[]{:T(256)} %constant.86.clone.1), dimensions={0}, to_apply=%region_6.7 | reduce | flops 1161216 | bytes 2985986 | tf_op jit(solution)/shard_map/reduce_sum | solution.py:135
  100.8 7.9 %all-to-all-start.1 = ((bf16[16,88,128]{2,1,0:T(8,128)(2,1)}), bf16[16,88,128]{2,1,0:T(8,128)(2,1)S(1)}, u32[]{:S(2)}, u32[]{:S(2)}) async-start(bf16[16,88,128]{2,1,0:T(8,128)(2,1)} %pad.9), calls=%async_computation.1 | async-start | bytes 720896 | tf_op jit(solution)/shard_map/all_to_all | solution.py:138
  109.3 12.0 %all-to-all-done.1 = bf16[16,88,128]{2,1,0:T(8,128)(2,1)S(1)} async-done(((bf16[16,88,128]{2,1,0:T(8,128)(2,1)}), bf16[16,88,128]{2,1,0:T(8,128)(2,1)S(1)}, u32[]{:S(2)}, u32[]{:S(2)}) %all-to-all-start.1) | async-done | bytes 360480 | tf_op jit(solution)/shard_map/all_to_all | solution.py:138
  (45 shorter events, 9.3 us)
Async XLA Ops:
  0.6 37.9 %copy-start = (bf16[1152,1152]{1,0:T(8,128)(2,1)S(1)}, bf16[1152,1152]{1,0:T(8,128)(2,1)}, u32[]{:S(2)}) copy-start(bf16[1152,1152]{1,0:T(8,128)(2,1)} %param.14) | copy-start | bytes 7962628
  0.6 29.1 %collective-permute-start.3 = (bf16[256,1152]{1,0:T(8,128)(2,1)}, bf16[256,1152]{1,0:T(8,128)(2,1)S(1)}, u32[]{:S(2)}, u32[]{:S(2)}) collective-permute-start(bf16[256,1152]{1,0:T(8,128)(2,1)} %bitcast.26), channel_id=1, source_target_pairs={{0,4},{1,5},{2,6},{3,7},{4,8},{5,9},{6,10},{7,11},{8,12},{9,13},{1... | collective-permute-start | bytes 1769480 | tf_op jit(solution)/shard_map/ppermute | solution.py:92
  4.3 4.9 %collective-permute-start.1 = (bf16[256,1152]{1,0:T(8,128)(2,1)}, bf16[256,1152]{1,0:T(8,128)(2,1)}, u32[]{:S(2)}, u32[]{:S(2)}) collective-permute-start(bf16[256,1152]{1,0:T(8,128)(2,1)} %bitcast.27), channel_id=1, source_target_pairs={{0,2},{1,3},{2,0},{3,1},{4,6},{5,7},{6,4},{7,5},{8,10},{9,11},{10,... | collective-permute-start | bytes 1769480 | tf_op jit(solution)/shard_map/ppermute | solution.py:90
  5.3 6.4 %collective-permute-start = (bf16[256,1152]{1,0:T(8,128)(2,1)}, bf16[256,1152]{1,0:T(8,128)(2,1)}, u32[]{:S(2)}, u32[]{:S(2)}) collective-permute-start(bf16[256,1152]{1,0:T(8,128)(2,1)} %bitcast.32), channel_id=1, source_target_pairs={{0,2},{1,3},{2,0},{3,1},{4,6},{5,7},{6,4},{7,5},{8,10},{9,11},{10,... | collective-permute-start | bytes 1769480 | tf_op jit(solution)/shard_map/ppermute | solution.py:90
  10.3 21.2 %collective-permute-start.2 = (bf16[128,1152]{1,0:T(8,128)(2,1)S(1)}, bf16[128,1152]{1,0:T(8,128)(2,1)S(1)}, u32[]{:S(2)}, u32[]{:S(2)}) collective-permute-start(bf16[128,1152]{1,0:T(8,128)(2,1)S(1)} %slice_select_fusion), channel_id=1, source_target_pairs={{0,8},{1,9},{2,10},{3,11},{4,12},{5,13},{6,14},{7,15},{8,16},{9,17... | collective-permute-start | bytes 884744 | tf_op jit(solution)/shard_map/ppermute | solution.py:94
  16.1 36.7 %copy-start.3 = (f32[512,1152]{1,0:T(8,128)}, f32[512,1152]{1,0:T(8,128)S(1)}, u32[]{:S(2)}) copy-start(f32[512,1152]{1,0:T(8,128)S(1)} %get-tuple-element.35) | copy-start | bytes 7077892
  31.6 3.7 %collective-permute-start.4 = (bf16[384,1152]{1,0:T(8,128)(2,1)S(1)}, bf16[384,1152]{1,0:T(8,128)(2,1)S(1)}, u32[]{:S(2)}, u32[]{:S(2)}) collective-permute-start(bf16[384,1152]{1,0:T(8,128)(2,1)S(1)} %pad_maximum_fusion.2), channel_id=1, source_target_pairs={{0,2},{1,3},{2,0},{3,1},{4,6},{5,7},{6,4},{7,5},{8,10},{9,11},{10,... | collective-permute-start | bytes 2654216 | tf_op jit(solution)/shard_map/ppermute | solution.py:90
  35.3 1.5 %copy-start.4 = (bf16[1,256,1152]{2,1,0:T(8,128)(2,1)S(1)}, bf16[1,256,1152]{2,1,0:T(8,128)(2,1)}, u32[]{:S(2)}) copy-start(bf16[1,256,1152]{2,1,0:T(8,128)(2,1)} %param.12) | copy-start | bytes 1769476
  37.0 5.8 %copy-start.7 = (bf16[1280,1152]{1,0:T(8,128)(2,1)}, bf16[1280,1152]{1,0:T(8,128)(2,1)S(1)}, u32[]{:S(2)}) copy-start(bf16[1280,1152]{1,0:T(8,128)(2,1)S(1)} %get-tuple-element.30) | copy-start | bytes 8847364
  38.5 4.2 %copy-start.8 = (bf16[1280,1152]{1,0:T(8,128)(2,1)}, bf16[1280,1152]{1,0:T(8,128)(2,1)S(1)}, u32[]{:S(2)}) copy-start(bf16[1280,1152]{1,0:T(8,128)(2,1)S(1)} %constant_dynamic-update-slice_fusion) | copy-start | bytes 8847364
  42.8 9.1 %copy-start.1 = (f32[1280,1152]{0,1:T(8,128)}, f32[1280,1152]{0,1:T(8,128)S(1)}, u32[]{:S(2)}) copy-start(f32[1280,1152]{0,1:T(8,128)S(1)} %get-tuple-element.33) | copy-start | bytes 17694724
  47.3 5.4 %copy-start.5 = (f32[256,1152]{1,0:T(8,128)}, f32[256,1152]{1,0:T(8,128)S(1)}, u32[]{:S(2)}) copy-start(f32[256,1152]{1,0:T(8,128)S(1)} %fusion.8) | copy-start | bytes 3538948
  49.6 3.2 %copy-start.6 = (f32[256,1152]{1,0:T(8,128)}, f32[256,1152]{1,0:T(8,128)S(1)}, u32[]{:S(2)}) copy-start(f32[256,1152]{1,0:T(8,128)S(1)} %fusion.4) | copy-start | bytes 3538948
  51.9 2.6 %copy-start.2 = (f32[1280,1152]{0,1:T(8,128)}, f32[1280,1152]{0,1:T(8,128)S(1)}, u32[]{:S(2)}) copy-start(f32[1280,1152]{0,1:T(8,128)S(1)} %fusion) | copy-start | bytes 17694724
  100.8 20.5 %all-to-all-start.1 = ((bf16[16,88,128]{2,1,0:T(8,128)(2,1)}), bf16[16,88,128]{2,1,0:T(8,128)(2,1)S(1)}, u32[]{:S(2)}, u32[]{:S(2)}) async-start(bf16[16,88,128]{2,1,0:T(8,128)(2,1)} %pad.9), calls=%async_computation.1 | async-start | bytes 720896 | tf_op jit(solution)/shard_map/all_to_all | solution.py:138

commit v2 on v1

v2 whole, which is shorter than its diff:
```python
import jax
import jax.numpy as jnp
from jax import lax
from jax.experimental import pallas as pl
from jax.experimental.pallas import tpu as pltpu
from jax.sharding import Mesh, PartitionSpec as P

AXES = ("z", "y", "xh", "c", "xl")
NZ, NY, NX = 8, 4, 4
BLOCK = 256
WIDTH = 1152
MIB = 1 << 20
BF16, F32 = jnp.bfloat16, jnp.float32


def place(i):
    return i // 32, (i // 8) % 4, ((i // 4) % 2) * 2 + i % 2, (i // 2) % 2


def index(z, y, x, c):
    return (((z * NY + y) * 2 + x // 2) * 2 + c) * 2 + x % 2


def chip_shift(by):
    pairs = []
    for i in range(256):
        z, y, x, c = place(i)
        q = (((z * NY + y) * 2 + x // 2) + by) % 64
        pairs.append((i, index(q // 8, (q // 2) % 4, (q % 2) * 2 + x % 2, c)))
    return pairs


def core_swap():
    return [(i, index(*place(i)[:3], 1 - place(i)[3])) for i in range(256)]


def grouped(key, order):
    found = {}
    for i in range(256):
        found.setdefault(key(*place(i)), []).append(i)
    return [sorted(v, key=lambda i: order(*place(i))) for v in found.values()]


def first_groups():
    return grouped(
        lambda z, y, x, c: (c, y, z // 2) if c == 0 else (c, x, ((z + 1) % NZ) // 2),
        lambda z, y, x, c: (z % 2, x if c == 0 else y),
    )


def second_groups():
    return grouped(
        lambda z, y, x, c: (c, x if c == 0 else y, z % 2),
        lambda z, y, x, c: (z // 2, y if c == 0 else x),
    )


def head_rows(c):
    r = lax.broadcasted_iota(jnp.int32, (576, 1), 0)

    def digit(r, size, count):
        d = sum((r >= size * k).astype(jnp.int32) for k in range(1, count))
        return d, r - size * d

    zl, r = digit(r, 288, 2)
    a, r = digit(r, 72, 4)
    zh, r = digit(r, 36, 2)
    b, r = digit(r, 9, 4)
    x, y = jnp.where(c == 0, a, b), jnp.where(c == 0, b, a)
    device = (((2 * zh + zl) * 4 + y) * 2 + (x >> 1)) * 4 + c * 2 + (x & 1)
    return 9 * device + r


def dot(a, b, contract=((1,), (0,))):
    return lax.dot_general(a, b, (contract, ((), ())), preferred_element_type=jnp.float32)


NT = ((1,), (1,))
TN = ((0,), (0,))


def normalise(feats, head):
    u = dot(feats, head)
    inv = lax.rsqrt(jnp.sum(u * u, axis=-1, keepdims=True) + 1e-06)
    return u * inv, inv


def rest(zf):
    return (zf - zf.astype(BF16).astype(F32)).astype(BF16)


def backnorm(grad, zfull, inv):
    return (inv * (grad - zfull * jnp.sum(grad * zfull, axis=-1, keepdims=True))).astype(BF16)


def score(query, keys, scale, bias, diagonal, gt_ref, loss_ref, wanted):
    logits = scale * dot(query, keys, NT) + bias
    if diagonal is not None:
        row = lax.broadcasted_iota(jnp.int32, logits.shape, 0)
        col = lax.broadcasted_iota(jnp.int32, logits.shape, 1)
        own = col == row + diagonal
        logits = jnp.where(own, -logits, logits)
    e = jnp.exp(-jnp.abs(logits))
    sig = jnp.where(logits >= 0, 1.0, e) / (1.0 + e)
    if diagonal is not None:
        sig = jnp.where(own, -sig, sig)
    gt_ref[...] = (scale * sig / BLOCK).astype(BF16)

    @pl.when(wanted)
    def _():
        loss_ref[...] += jnp.sum(jnp.maximum(logits, 0.0) + jnp.log1p(e), axis=1, keepdims=True)


def early_kernel(
    core_ref, par_ref, img, txt, oimg, otxt, himg_hbm, htxt_hbm,
    zi, lzi, inv, dq, fti, pick, loss, z4, lz4, inv4, g4, ft34, du3,
    himg, htxt, fimg, ftxt, zt, zf3, gts, sems,
):
    c = core_ref[0]
    mine, other = pl.multiple_of(c * BLOCK, BLOCK), pl.multiple_of((1 - c) * BLOCK, BLOCK)
    copies = [
        pltpu.make_async_copy(src, dst, sems.at[k])
        for k, (src, dst) in enumerate((
            (img, fimg.at[pl.ds(mine, BLOCK)]), (oimg, fimg.at[pl.ds(other, BLOCK)]), (himg_hbm, himg),
            (txt, ftxt.at[pl.ds(mine, BLOCK)]), (otxt, ftxt.at[pl.ds(other, BLOCK)]), (htxt_hbm, htxt),
        ))
    ]
    for copy in copies:
        copy.start()
    scale, bias = par_ref[0], par_ref[1]
    pick[...] = (lax.broadcasted_iota(jnp.int32, (576, WIDTH), 1) == head_rows(c)).astype(BF16)
    loss[...] = jnp.zeros_like(loss)
    lo, hi = slice(0, BLOCK), slice(BLOCK, 2 * BLOCK)
    for copy in copies[:3]:
        copy.wait()
    fti[...] = dot(pick[...], fimg[...], NT).astype(BF16)
    for rows in (lo, hi):
        zf, i = normalise(fimg[rows], himg[...])
        lzi[rows] = rest(zf)
        zi[rows] = zf.astype(BF16)
        inv[rows] = i
    for copy in copies[3:]:
        copy.wait()
    ft34[...] = dot(pick[...], ftxt[...], NT).astype(BF16)
    zf, inv3 = normalise(ftxt[lo], htxt[...])
    zf3[...] = zf
    zt[lo] = zf.astype(BF16)
    zf, i = normalise(ftxt[hi], htxt[...])
    lz4[...] = rest(zf)
    zt[hi] = zf.astype(BF16)
    z4[...] = zt[hi]
    inv4[...] = i
    score(zi[lo], zt[lo], scale, bias, 0, gts.at[lo, lo], loss, c == 0)
    score(zi[hi], zt[...], scale, bias, BLOCK, gts.at[hi, :], loss, c == 1)
    dq[lo] = dot(gts[lo, lo], zt[lo])
    dq[hi] = dot(gts[hi, :], zt[...])
    du3[...] = backnorm(dot(gts[:, lo], zi[...], TN), zf3[...], inv3)
    g4[...] = dot(gts[hi, hi], zi[hi], TN)


def late_kernel(
    core_ref, par_ref, near, near_o, far, far_o,
    himg, htxt, zi, lzi, inv, dq, fti, pick, loss_near, z4, lz4, inv4, g4, ft34, du3,
    out, loss_out, loss_far,
    ft, f2, zt, zft, z2, zf2, gts, gt2, loss, loss2, du_i, du_t, ftt, ft2,
):
    c = core_ref[0]
    f2[pl.ds(pl.multiple_of(c * 128, 128), 128)] = far[...]
    f2[pl.ds(pl.multiple_of((1 - c) * 128, 128), 128)] = far_o[...]
    ft[pl.ds(pl.multiple_of(c * BLOCK, BLOCK), BLOCK)] = near[...]
    ft[pl.ds(pl.multiple_of((1 - c) * BLOCK, BLOCK), BLOCK)] = near_o[...]
    scale, bias = par_ref[0], par_ref[1]
    lo, hi, end = slice(0, BLOCK), slice(BLOCK, 2 * BLOCK), slice(2 * BLOCK, 3 * BLOCK)
    zf, inv2 = normalise(f2[...], himg[...])
    zf2[...] = zf
    z2[...] = zf.astype(BF16)
    inv_t = []
    for rows in (lo, hi):
        zf, i = normalise(ft[rows], htxt[...])
        zft[rows] = zf
        zt[rows] = zf.astype(BF16)
        inv_t.append(i)
    ft2[...] = dot(pick[...], f2[...], NT).astype(BF16)
    ftt[...] = dot(pick[...], ft[...], NT).astype(BF16)
    loss[...] = loss_near[...]
    loss2[...] = jnp.zeros_like(loss2)
    score(z2[...], z4[...], scale, bias, None, gt2, loss2, c == 0)
    score(zi[lo], zt[...], scale, bias, None, gts.at[lo, :], loss, c == 0)
    score(zi[hi], zt[...], scale, bias, None, gts.at[hi, :], loss, c == 1)
    loss_out[...] = jnp.transpose(jnp.broadcast_to(loss[...], (BLOCK, 128)))[:1]
    loss_far[...] = jnp.transpose(jnp.broadcast_to(loss2[...], (BLOCK, 128)))[:1]
    du_i[end] = backnorm(dot(gt2[...], z4[...]), zf2[...], inv2)
    du_t[2 * BLOCK : 3 * BLOCK] = du3[...]
    du_t[3 * BLOCK :] = backnorm(g4[...] + dot(gt2[...], z2[...], TN), z4[...].astype(F32) + lz4[...], inv4[...])
    for rows, inv_k in zip((lo, hi), inv_t):
        du_i[rows] = backnorm(dq[rows] + dot(gts[rows, :], zt[...]), zi[rows].astype(F32) + lzi[rows], inv[rows])
        du_t[rows] = backnorm(dot(gts[:, rows], zi[...], TN), zft[rows], inv_k)
    for first in range(0, WIDTH, 256):
        cols = slice(first, min(first + 256, WIDTH))
        g_i = dot(fti[...], du_i[: 2 * BLOCK, cols]) + dot(ft2[...], du_i[end, cols])
        g_t = dot(ftt[...], du_t[: 2 * BLOCK, cols]) + dot(ft34[...], du_t[2 * BLOCK :, cols])
        wide = g_i.shape[1]
        both = jnp.concatenate([g_i.reshape(8, 72, wide), g_t.reshape(8, 72, wide)], axis=1)
        out[:, cols] = both.reshape(WIDTH, wide).astype(BF16)


def half_kernel(got, out, total, parts):
    acc = got[0:144].astype(F32)
    for j in range(1, 8):
        acc += got[144 * j : 144 * (j + 1)].astype(F32)
    total[...] = acc
    parts[...] = jnp.zeros_like(parts)
    for m in range(16):
        for l in range(9):
            parts[88 * m + 9 * l : 88 * m + 9 * l + 9] = total[9 * m : 9 * m + 9, 128 * l : 128 * (l + 1)]
    out[...] = parts[...].astype(BF16)


def last_kernel(core_ref, got, loss, loss_far, out, loss_out, total):
    values = got[...].astype(F32)
    acc = values[:88]
    for j in range(1, 16):
        acc += values[88 * j : 88 * (j + 1)]
    total[...] = acc
    for l in range(9):
        out[:, 128 * l : 128 * (l + 1)] = total[9 * l : 9 * l + 9]
    loss_out[...] = loss[...] + jnp.where(core_ref[0] == 0, loss_far[...], 0.0)


def call(kernel, out_shape, scratch, flops, spaces, limit=24 * MIB):
    vmem = pl.BlockSpec(memory_space=pltpu.VMEM)
    spec = {"s": pl.BlockSpec(memory_space=pltpu.SMEM), "v": vmem, "h": pl.BlockSpec(memory_space=pltpu.HBM)}
    return pl.pallas_call(
        kernel,
        out_shape=out_shape,
        in_specs=[spec[k] for k in spaces],
        out_specs=jax.tree.map(lambda _: vmem, out_shape),
        scratch_shapes=scratch,
        compiler_params=pltpu.CompilerParams(vmem_limit_bytes=limit),
        cost_estimate=pl.CostEstimate(flops=flops, bytes_accessed=8 * MIB, transcendentals=0),
    )


def shapes(dtype, *dims):
    return [jax.ShapeDtypeStruct(d, dtype) for d in dims]


def scratches(dtype, *dims):
    return [pltpu.VMEM(d, dtype) for d in dims]


def local(images, texts, img_head, txt_head, log_scale, bias):
    img, txt = images[0], texts[0]
    c = lax.axis_index("c")
    first = c == 0
    core = jnp.reshape(c, (1,)).astype(jnp.int32)
    params = jnp.stack([jnp.exp(log_scale), bias])

    def swap(a):
        return lax.ppermute(a, AXES, core_swap())

    near = lax.ppermute(txt, AXES, chip_shift(1))
    other_img = swap(img)
    far = lax.ppermute(jnp.where(first, img[:128], other_img[128:]), AXES, chip_shift(-2))
    other_txt = swap(txt)

    one, two, three = (BLOCK, WIDTH), (2 * BLOCK, WIDTH), (3 * BLOCK, WIDTH)
    square, head, column = (WIDTH, WIDTH), (576, WIDTH), (BLOCK, 1)
    kept = call(
        early_kernel,
        shapes(BF16, two, two) + shapes(F32, (512, 1), two) + shapes(BF16, (576, 512))
        + shapes(BF16, head) + shapes(F32, column) + shapes(BF16, one, one)
        + shapes(F32, column, one) + shapes(BF16, (576, 512), one),
        scratches(BF16, square, square, two, two, two) + scratches(F32, one)
        + scratches(BF16, (512, 512)) + [pltpu.SemaphoreType.DMA((6,))],
        2 * 9 * 340_000_000, "ssvvvvhh", 40 * MIB,
    )(core, params, img, txt, other_img, other_txt, img_head, txt_head)

    near, far, *kept = lax.optimization_barrier((near, far, *kept))
    near_o, far_o = swap(near), swap(far)
    term, loss, loss_far = call(
        late_kernel,
        shapes(BF16, square) + shapes(F32, (1, BLOCK), (1, BLOCK)),
        scratches(BF16, two, one, two) + scratches(F32, two) + scratches(BF16, one) + scratches(F32, one)
        + scratches(BF16, (512, 512), (BLOCK, BLOCK)) + scratches(F32, column, column)
        + scratches(BF16, three, (4 * BLOCK, WIDTH), (576, 512), (576, BLOCK)),
        2 * 10 * 340_000_000, "ss" + "v" * 19,
    )(core, params, near, near_o, far, far_o, img_head, txt_head, *kept)

    loss_far = lax.ppermute(loss_far, AXES, chip_shift(2))
    got = lax.all_to_all(term, AXES, 0, 0, axis_index_groups=first_groups(), tiled=True)
    (half,) = call(
        half_kernel, shapes(BF16, (1408, 128)), scratches(F32, (144, WIDTH), (1408, 128)), 10_000_000, "v",
    )(got)
    got = lax.all_to_all(half, AXES, 0, 0, axis_index_groups=second_groups(), tiled=True)
    shares, loss = call(
        last_kernel, shapes(F32, (9, WIDTH), (1, BLOCK)), scratches(F32, (88, 128)), 1_000_000, "svvv",
    )(core, got, loss, loss_far)
    return (loss, shares)


def solution(mesh):
    inner = Mesh(mesh.devices.reshape(NZ, NY, 2, 2, 2), AXES)
    dp = ("z", "y", "xh", "c")
    placed = (P("xl", dp, None), P("xl", dp, None), P(), P(), P(), P())
    return jax.shard_map(
        local,
        mesh=inner,
        in_specs=placed,
        out_specs=(P("xl", dp), P(AXES, None)),
        check_vma=False,
    )
```

time: 122 us -> 89.9 us (0.74)
  matrix products: 33.8 us -> 0 us
  Pallas kernels: 0 us -> 27.3 us
  waiting for transfers between devices: 29.2 us -> 14.8 us
  other arithmetic: 9.67 us -> 1.07 us
  local copies, waits for them, and re-layouts: 7.94 us -> 2.14 us
  starting transfers between devices: 15.5 us -> 19.5 us
    dot_general x10 -> x0, matrix products: 33.8 us -> none  [the longest x2 17.2 us: local(): jnp.dot(ft, du, preferred_element_type=jnp.float32).reshape(8, 72, 1152)]
    pallas_call x0 -> x4, Pallas kernels: none -> 27.3 us  [the longest x1 13.4 us: local(): call(late_kernel, shapes(BF16, square) + shapes(F32, (1, BLOCK), (1, BLOC...]
    ppermute x1, waiting for transfers between devices: 13.7 us -> 0.01 us  [local(): near = lax.ppermute(txt, AXES, chip_shift(1))]
    ppermute x1 -> x2, starting transfers between devices: 1.37 us -> 8.47 us  [the longest x1 8.1 us: local(): lax.ppermute(jnp.where(first, img[:128], other_img[128:]), AXES, chip_shi...]
    all_to_all x1, waiting for transfers between devices: 12 us -> 7.44 us  [local(): lax.all_to_all(half, AXES, 0, 0, axis_index_groups=second_groups(), tiled...]
    ppermute x1 -> x2, waiting for transfers between devices: 1.78 us -> 5.56 us  [the longest x1 5.56 us: local(): loss_far = lax.ppermute(loss_far, AXES, chip_shift(2))]
    reduce_sum x4 -> x0, other arithmetic: 3.44 us -> none  [the longest x1 2.17 us: local(): half = jnp.sum(got.reshape(8, 16, 9, 1152).astype(jnp.float32), axis=0)]
    ppermute x1, starting transfers between devices: 3.65 us -> 1.01 us  [local(): near = lax.ppermute(txt, AXES, chip_shift(1))]
  transfers between devices with their start and end apart: 6 -> 8, of which waited for: 4 -> 3; matrix products, arithmetic and copies ran while one was open for 7% -> 1% of each run, Pallas kernels for 0% -> 13%
where the time goes in v2:
time: 89.9 us; the launch traced here: 89.5 us
  Pallas kernels  27.3 us (30%)
  blocking collectives  22.8 us (25%)
  starting transfers between devices  19.5 us (22%)
  waiting for transfers between devices  14.8 us (16%)
  local copies, waits for them, and re-layouts  2.14 us (2%)
  between operations  2.02 us (2%)
  other arithmetic  1.07 us (1%)
    all_to_all x1, blocking collectives, local(): lax.all_to_all(term, AXES, 0, 0, axis_index_groups=first_groups(), tiled=...  22.8 us
    pallas_call x1, Pallas kernels, local(): call(late_kernel, shapes(BF16, square) + shapes(F32, (1, BLOCK), (1, BLOC...  13.4 us
    pallas_call x1, Pallas kernels, local(): call(early_kernel, shapes(BF16, two, two) + shapes(F32, (512, 1), two) +...  11.7 us
    ppermute x1, starting transfers between devices, local(): lax.ppermute(jnp.where(first, img[:128], other_img[128:]), AXES, chip_shi...  8.1 us
    all_to_all x1, waiting for transfers between devices, local(): lax.all_to_all(half, AXES, 0, 0, axis_index_groups=second_groups(), tiled...  7.44 us
    ppermute x1, waiting for transfers between devices, local(): loss_far = lax.ppermute(loss_far, AXES, chip_shift(2))  5.56 us
    all_to_all x1, starting transfers between devices, local(): lax.all_to_all(half, AXES, 0, 0, axis_index_groups=second_groups(), tiled...  5.34 us
    ppermute x4, starting transfers between devices, swap(): return lax.ppermute(a, AXES, core_swap())  4.66 us
  transfers between devices with their start and end apart: 8, of which 3 were waited for; matrix products, arithmetic and copies ran while one was open for 1% of the time, Pallas kernels for 13%

profile of v2, /device:TPU:1, one launch (start us, length us, event | category | flops | bytes accessed | tf_op | source)
XLA Modules:
  0.0 89.5 jit_solution(3353375401159802308)
XLA Ops:
  0.6 3.3 %collective-permute-start.1 = (bf16[256,1152]{1,0:T(8,128)(2,1)}, bf16[256,1152]{1,0:T(8,128)(2,1)S(1)}, u32[]{:S(2)}, u32[]{:S(2)}) collective-permute-start(bf16[256,1152]{1,0:T(8,128)(2,1)} %bitcast.15), channel_id=1, source_target_pairs={{0,2},{1,3},{2,0},{3,1},{4,6},{5,7},{6,4},{7,5},{8,10},{9,11},{10,... | collective-permute-start | bytes 1769480 | tf_op jit(solution)/shard_map/ppermute | solution.py:260
  4.0 0.1 collective-permute-start.3
  4.1 1.0 %collective-permute-start = (bf16[256,1152]{1,0:T(8,128)(2,1)}, bf16[256,1152]{1,0:T(8,128)(2,1)S(1)}, u32[]{:S(2)}, u32[]{:S(2)}) collective-permute-start(bf16[256,1152]{1,0:T(8,128)(2,1)} %bitcast.18), channel_id=1, source_target_pairs={{0,4},{1,5},{2,6},{3,7},{4,8},{5,9},{6,10},{7,11},{8,12},{9,13},{1... | collective-permute-start | bytes 1769480 | tf_op jit(solution)/shard_map/ppermute | solution.py:262
  6.4 0.1 pad_maximum_fusion.par_ref
  6.5 0.0 collective-permute-done.1.oimg
  6.5 1.0 %slice_select_fusion = bf16[128,1152]{1,0:T(8,128)(2,1)S(1)} fusion(bf16[256,1152]{1,0:T(8,128)(2,1)S(1)} %collective-permute-done.1.oimg, bf16[1,256,1152]{2,1,0:T(8,128)(2,1)} %param.6, pred[]{:T(512)S(6)} %eq.3), kind=kLoop, calls=%fused_computation | loop fusion | flops 147456 | bytes 884737 | tf_op jit(solution)/shard_map/jit(_where)/select_n | solution.py:264
  7.5 8.1 %collective-permute-start.2 = (bf16[128,1152]{1,0:T(8,128)(2,1)S(1)}, bf16[128,1152]{1,0:T(8,128)(2,1)S(1)}, u32[]{:S(2)}, u32[]{:S(2)}) collective-permute-start(bf16[128,1152]{1,0:T(8,128)(2,1)S(1)} %slice_select_fusion), channel_id=1, source_target_pairs={{0,248},{1,249},{2,250},{3,251},{4,252},{5,253},{6,254},{7,255},{8... | collective-permute-start | bytes 884744 | tf_op jit(solution)/shard_map/ppermute | solution.py:264
  15.6 0.0 collective-permute-done.3.otxt
  15.6 1.1 %copy-done = bf16[1,256,1152]{2,1,0:T(8,128)(2,1)S(1)} copy-done((bf16[1,256,1152]{2,1,0:T(8,128)(2,1)S(1)}, bf16[1,256,1152]{2,1,0:T(8,128)(2,1)}, u32[]{:S(2)}) %copy-start) | copy-done | bytes 589848
  16.7 1.1 %copy-done.3 = bf16[1,256,1152]{2,1,0:T(8,128)(2,1)S(1)} copy-done((bf16[1,256,1152]{2,1,0:T(8,128)(2,1)S(1)}, bf16[1,256,1152]{2,1,0:T(8,128)(2,1)}, u32[]{:S(2)}) %copy-start.3) | copy-done | bytes 589848
  17.7 11.7 %shard_map.77 = (bf16[512,1152]{1,0:T(8,128)(2,1)S(1)}, bf16[512,1152]{1,0:T(8,128)(2,1)S(1)}, f32[512,1]{1,0:T(8,128)S(1)}, f32[512,1152]{1,0:T(8,128)S(1)}, bf...) custom-call(s32[1]{0:T(128)} %bitcast.core_ref, ...), custom_call_target="tpu_custom_call" | custom-call | flops 6120000000 | bytes 8388608 | tf_op jit(solution)/shard_map/pallas_call | solution.py:269
  29.4 0.0 collective-permute-done.near
  29.5 1.0 %collective-permute-start.4 = (bf16[256,1152]{1,0:T(8,128)(2,1)S(1)}, bf16[256,1152]{1,0:T(8,128)(2,1)S(1)}, u32[]{:S(2)}, u32[]{:S(2)}) collective-permute-start(bf16[256,1152]{1,0:T(8,128)(2,1)S(1)} %collective-permute-done.near), channel_id=1, source_target_pairs={{0,2},{1,3},{2,0},{3,1},{4,6},{5,7},{6,4},{7,5},{8,10},{9,11},{10,... | collective-permute-start | bytes 1769480 | tf_op jit(solution)/shard_map/ppermute | solution.py:260
  30.4 0.3 collective-permute-start.5
  30.7 1.8 %collective-permute-done.5.far_o = bf16[128,1152]{1,0:T(8,128)(2,1)S(1)} collective-permute-done((bf16[128,1152]{1,0:T(8,128)(2,1)S(1)}, bf16[128,1152]{1,0:T(8,128)(2,1)S(1)}, u32[]{:S(2)}, u32[]{:S(2)}) %collective-permute-start.5) | collective-permute-done | bytes 294944 | tf_op jit(solution)/shard_map/ppermute | solution.py:260
  32.5 0.0 collective-permute-done.4.near_o
  32.5 13.4 %shard_map.78 = (bf16[1152,1152]{1,0:T(8,128)(2,1)S(1)}, f32[1,256]{1,0:T(1,128)S(1)}, f32[1,256]{1,0:T(1,128)S(1)}) custom-call(s32[1]{0:T(128)} %bitcast.core_ref, f32[2]{0:T(128)S(1)} %pad_maximum_fusion.par_ref, bf16[256,1152]{1,0:T(8,128)(2,1)S(1)} %collective-permute-done.near, bf16[256,1152]{1,0:T(8,128)(2,1)S(1)} %collective-permute-done.4.near_o, ...), custom_call_target="tpu_custom_call" | custom-call | flops 6800000000 | bytes 8388608 | tf_op jit(solution)/shard_map/pallas_call | solution.py:281
  45.9 22.8 %all_to_all.22 = bf16[8,144,1152]{2,1,0:T(8,128)(2,1)S(1)} all-to-all(bf16[8,144,1152]{2,1,0:T(8,128)(2,1)S(1)} %bitcast.13), channel_id=1, replica_groups={{0,1,4,5,32,33,36,37},{2,10,18,26,226,234,242,250},{3,11,19,27,227,235,..., dimensions={0} | all-to-all | bytes 5308416 | tf_op jit(solution)/shard_map/all_to_all | solution.py:291
  68.7 1.5 %shard_map.79 = bf16[1408,128]{1,0:T(8,128)(2,1)} custom-call(bf16[1152,1152]{1,0:T(8,128)(2,1)S(1)} %bitcast.12), custom_call_target="tpu_custom_call" | custom-call | flops 10000000 | bytes 8388608 | tf_op jit(solution)/shard_map/pallas_call | solution.py:292
  70.1 5.3 %all-to-all-start.1 = ((bf16[16,88,128]{2,1,0:T(8,128)(2,1)}), bf16[16,88,128]{2,1,0:T(8,128)(2,1)S(1)}, u32[]{:S(2)}, u32[]{:S(2)}) async-start(bf16[16,88,128]{2,1,0:T(8,128)(2,1)} %bitcast.8), calls=%async_computation.1 | async-start | bytes 720896 | tf_op jit(solution)/shard_map/all_to_all | solution.py:295
  75.5 0.4 collective-permute-start.6
  75.8 5.6 %collective-permute-done.6.loss_far = f32[1,256]{1,0:T(1,128)S(1)} collective-permute-done((f32[1,256]{1,0:T(1,128)S(1)}, f32[1,256]{1,0:T(1,128)S(1)}, u32[]{:S(2)}, u32[]{:S(2)}) %collective-permute-start.6) | collective-permute-done | bytes 1056 | tf_op jit(solution)/shard_map/ppermute | solution.py:290
  81.4 7.4 %all-to-all-done.1 = bf16[16,88,128]{2,1,0:T(8,128)(2,1)S(1)} async-done(((bf16[16,88,128]{2,1,0:T(8,128)(2,1)}), bf16[16,88,128]{2,1,0:T(8,128)(2,1)S(1)}, u32[]{:S(2)}, u32[]{:S(2)}) %all-to-all-start.1) | async-done | bytes 360480 | tf_op jit(solution)/shard_map/all_to_all | solution.py:295
  88.8 0.7 shard_map.80
  (7 shorter events, 0.0 us)
Async XLA Ops:
  0.6 5.9 %collective-permute-start.1 = (bf16[256,1152]{1,0:T(8,128)(2,1)}, bf16[256,1152]{1,0:T(8,128)(2,1)S(1)}, u32[]{:S(2)}, u32[]{:S(2)}) collective-permute-start(bf16[256,1152]{1,0:T(8,128)(2,1)} %bitcast.15), channel_id=1, source_target_pairs={{0,2},{1,3},{2,0},{3,1},{4,6},{5,7},{6,4},{7,5},{8,10},{9,11},{10,... | collective-permute-start | bytes 1769480 | tf_op jit(solution)/shard_map/ppermute | solution.py:260
  4.0 11.6 %collective-permute-start.3 = (bf16[256,1152]{1,0:T(8,128)(2,1)}, bf16[256,1152]{1,0:T(8,128)(2,1)S(1)}, u32[]{:S(2)}, u32[]{:S(2)}) collective-permute-start(bf16[256,1152]{1,0:T(8,128)(2,1)} %bitcast.17), channel_id=1, source_target_pairs={{0,2},{1,3},{2,0},{3,1},{4,6},{5,7},{6,4},{7,5},{8,10},{9,11},{10,... | collective-permute-start | bytes 1769480 | tf_op jit(solution)/shard_map/ppermute | solution.py:260
  4.1 25.4 %collective-permute-start = (bf16[256,1152]{1,0:T(8,128)(2,1)}, bf16[256,1152]{1,0:T(8,128)(2,1)S(1)}, u32[]{:S(2)}, u32[]{:S(2)}) collective-permute-start(bf16[256,1152]{1,0:T(8,128)(2,1)} %bitcast.18), channel_id=1, source_target_pairs={{0,4},{1,5},{2,6},{3,7},{4,8},{5,9},{6,10},{7,11},{8,12},{9,13},{1... | collective-permute-start | bytes 1769480 | tf_op jit(solution)/shard_map/ppermute | solution.py:262
  7.5 22.0 %collective-permute-start.2 = (bf16[128,1152]{1,0:T(8,128)(2,1)S(1)}, bf16[128,1152]{1,0:T(8,128)(2,1)S(1)}, u32[]{:S(2)}, u32[]{:S(2)}) collective-permute-start(bf16[128,1152]{1,0:T(8,128)(2,1)S(1)} %slice_select_fusion), channel_id=1, source_target_pairs={{0,248},{1,249},{2,250},{3,251},{4,252},{5,253},{6,254},{7,255},{8... | collective-permute-start | bytes 884744 | tf_op jit(solution)/shard_map/ppermute | solution.py:264
  15.6 1.1 %copy-start = (bf16[1,256,1152]{2,1,0:T(8,128)(2,1)S(1)}, bf16[1,256,1152]{2,1,0:T(8,128)(2,1)}, u32[]{:S(2)}) copy-start(bf16[1,256,1152]{2,1,0:T(8,128)(2,1)} %param.6) | copy-start | bytes 1769476
  16.7 1.1 %copy-start.3 = (bf16[1,256,1152]{2,1,0:T(8,128)(2,1)S(1)}, bf16[1,256,1152]{2,1,0:T(8,128)(2,1)}, u32[]{:S(2)}) copy-start(bf16[1,256,1152]{2,1,0:T(8,128)(2,1)} %param.7) | copy-start | bytes 1769476
  17.7 14.7 %copy-start.1 = (bf16[1152,1152]{1,0:T(8,128)(2,1)S(1)}, bf16[1152,1152]{1,0:T(8,128)(2,1)}, u32[]{:S(2)}) copy-start(bf16[1152,1152]{1,0:T(8,128)(2,1)} %himg.1) | copy-start | bytes 7962628
  17.7 14.7 %copy-start.2 = (bf16[1152,1152]{1,0:T(8,128)(2,1)S(1)}, bf16[1152,1152]{1,0:T(8,128)(2,1)}, u32[]{:S(2)}) copy-start(bf16[1152,1152]{1,0:T(8,128)(2,1)} %htxt.1) | copy-start | bytes 7962628
  29.5 3.0 %collective-permute-start.4 = (bf16[256,1152]{1,0:T(8,128)(2,1)S(1)}, bf16[256,1152]{1,0:T(8,128)(2,1)S(1)}, u32[]{:S(2)}, u32[]{:S(2)}) collective-permute-start(bf16[256,1152]{1,0:T(8,128)(2,1)S(1)} %collective-permute-done.near), channel_id=1, source_target_pairs={{0,2},{1,3},{2,0},{3,1},{4,6},{5,7},{6,4},{7,5},{8,10},{9,11},{10,... | collective-permute-start | bytes 1769480 | tf_op jit(solution)/shard_map/ppermute | solution.py:260
  30.4 2.1 %collective-permute-start.5 = (bf16[128,1152]{1,0:T(8,128)(2,1)S(1)}, bf16[128,1152]{1,0:T(8,128)(2,1)S(1)}, u32[]{:S(2)}, u32[]{:S(2)}) collective-permute-start(bf16[128,1152]{1,0:T(8,128)(2,1)S(1)} %collective-permute-done.2.far), channel_id=1, source_target_pairs={{0,2},{1,3},{2,0},{3,1},{4,6},{5,7},{6,4},{7,5},{8,10},{9,11},{10,... | collective-permute-start | bytes 884744 | tf_op jit(solution)/shard_map/ppermute | solution.py:260
  70.1 18.7 %all-to-all-start.1 = ((bf16[16,88,128]{2,1,0:T(8,128)(2,1)}), bf16[16,88,128]{2,1,0:T(8,128)(2,1)S(1)}, u32[]{:S(2)}, u32[]{:S(2)}) async-start(bf16[16,88,128]{2,1,0:T(8,128)(2,1)} %bitcast.8), calls=%async_computation.1 | async-start | bytes 720896 | tf_op jit(solution)/shard_map/all_to_all | solution.py:295
  75.5 5.9 %collective-permute-start.6 = (f32[1,256]{1,0:T(1,128)S(1)}, f32[1,256]{1,0:T(1,128)S(1)}, u32[]{:S(2)}, u32[]{:S(2)}) collective-permute-start(f32[1,256]{1,0:T(1,128)S(1)} %get-tuple-element.65), channel_id=1, source_target_pairs={{0,8},{1,9},{2,10},{3,11},{4,12},{5,13},{6,14},{7,15},{8,16},{9,17... | collective-permute-start | bytes 3080 | tf_op jit(solution)/shard_map/ppermute | solution.py:290

commit v3 on v2

--- a/solution.py
+++ b/solution.py
@@ -111,10 +111,13 @@
         loss_ref[...] += jnp.sum(jnp.maximum(logits, 0.0) + jnp.log1p(e), axis=1, keepdims=True)
 
 
+LO, HI, END = (slice(k * BLOCK, (k + 1) * BLOCK) for k in range(3))
+
+
 def early_kernel(
     core_ref, par_ref, img, txt, oimg, otxt, himg_hbm, htxt_hbm,
-    zi, lzi, inv, dq, fti, pick, loss, z4, lz4, inv4, g4, ft34, du3,
-    himg, htxt, fimg, ftxt, zt, zf3, gts, sems,
+    zi, lzi, inv, fti, pick, zt, lzt, invt, ft34,
+    himg, htxt, fimg, ftxt, sems,
 ):
     c = core_ref[0]
     mine, other = pl.multiple_of(c * BLOCK, BLOCK), pl.multiple_of((1 - c) * BLOCK, BLOCK)
@@ -127,40 +130,34 @@
     ]
     for copy in copies:
         copy.start()
+    pick[...] = (lax.broadcasted_iota(jnp.int32, (576, WIDTH), 1) == head_rows(c)).astype(BF16)
+    for f, ft, head, z, lz, i, waits in (
+        (fimg, fti, himg, zi, lzi, inv, copies[:3]), (ftxt, ft34, htxt, zt, lzt, invt, copies[3:]),
+    ):
+        for copy in waits:
+            copy.wait()
+        ft[...] = dot(pick[...], f[...], NT).astype(BF16)
+        for rows in (LO, HI):
+            zf, i[rows] = normalise(f[rows], head[...])
+            lz[rows] = rest(zf)
+            z[rows] = zf.astype(BF16)
+
+
+def own_kernel(core_ref, par_ref, zi, zt, lzt, invt, loss, dq, g4, du3, gts):
+    c = core_ref[0]
     scale, bias = par_ref[0], par_ref[1]
-    pick[...] = (lax.broadcasted_iota(jnp.int32, (576, WIDTH), 1) == head_rows(c)).astype(BF16)
     loss[...] = jnp.zeros_like(loss)
-    lo, hi = slice(0, BLOCK), slice(BLOCK, 2 * BLOCK)
-    for copy in copies[:3]:
-        copy.wait()
-    fti[...] = dot(pick[...], fimg[...], NT).astype(BF16)
-    for rows in (lo, hi):
-        zf, i = normalise(fimg[rows], himg[...])
-        lzi[rows] = rest(zf)
-        zi[rows] = zf.astype(BF16)
-        inv[rows] = i
-    for copy in copies[3:]:
-        copy.wait()
-    ft34[...] = dot(pick[...], ftxt[...], NT).astype(BF16)
-    zf, inv3 = normalise(ftxt[lo], htxt[...])
-    zf3[...] = zf
-    zt[lo] = zf.astype(BF16)
-    zf, i = normalise(ftxt[hi], htxt[...])
-    lz4[...] = rest(zf)
-    zt[hi] = zf.astype(BF16)
-    z4[...] = zt[hi]
-    inv4[...] = i
-    score(zi[lo], zt[lo], scale, bias, 0, gts.at[lo, lo], loss, c == 0)
-    score(zi[hi], zt[...], scale, bias, BLOCK, gts.at[hi, :], loss, c == 1)
-    dq[lo] = dot(gts[lo, lo], zt[lo])
-    dq[hi] = dot(gts[hi, :], zt[...])
-    du3[...] = backnorm(dot(gts[:, lo], zi[...], TN), zf3[...], inv3)
-    g4[...] = dot(gts[hi, hi], zi[hi], TN)
+    score(zi[LO], zt[LO], scale, bias, 0, gts.at[LO, LO], loss, c == 0)
+    score(zi[HI], zt[...], scale, bias, BLOCK, gts.at[HI, :], loss, c == 1)
+    dq[LO] = dot(gts[LO, LO], zt[LO])
+    dq[HI] = dot(gts[HI, :], zt[...])
+    du3[...] = backnorm(dot(gts[:, LO], zi[...], TN), zt[LO].astype(F32) + lzt[LO], invt[LO])
+    g4[...] = dot(gts[HI, HI], zi[HI], TN)
 
 
 def late_kernel(
     core_ref, par_ref, near, near_o, far, far_o,
-    himg, htxt, zi, lzi, inv, dq, fti, pick, loss_near, z4, lz4, inv4, g4, ft34, du3,
+    himg, htxt, zi, lzi, inv, fti, pick, zown, lzown, invown, ft34, loss_near, dq, g4, du3,
     out, loss_out, loss_far,
     ft, f2, zt, zft, z2, zf2, gts, gt2, loss, loss2, du_i, du_t, ftt, ft2,
 ):
@@ -184,14 +181,14 @@
     ftt[...] = dot(pick[...], ft[...], NT).astype(BF16)
     loss[...] = loss_near[...]
     loss2[...] = jnp.zeros_like(loss2)
-    score(z2[...], z4[...], scale, bias, None, gt2, loss2, c == 0)
+    score(z2[...], zown[HI], scale, bias, None, gt2, loss2, c == 0)
     score(zi[lo], zt[...], scale, bias, None, gts.at[lo, :], loss, c == 0)
     score(zi[hi], zt[...], scale, bias, None, gts.at[hi, :], loss, c == 1)
     loss_out[...] = jnp.transpose(jnp.broadcast_to(loss[...], (BLOCK, 128)))[:1]
     loss_far[...] = jnp.transpose(jnp.broadcast_to(loss2[...], (BLOCK, 128)))[:1]
-    du_i[end] = backnorm(dot(gt2[...], z4[...]), zf2[...], inv2)
+    du_i[end] = backnorm(dot(gt2[...], zown[HI]), zf2[...], inv2)
     du_t[2 * BLOCK : 3 * BLOCK] = du3[...]
-    du_t[3 * BLOCK :] = backnorm(g4[...] + dot(gt2[...], z2[...], TN), z4[...].astype(F32) + lz4[...], inv4[...])
+    du_t[3 * BLOCK :] = backnorm(g4[...] + dot(gt2[...], z2[...], TN), zown[HI].astype(F32) + lzown[HI], invown[HI])
     for rows, inv_k in zip((lo, hi), inv_t):
         du_i[rows] = backnorm(dq[rows] + dot(gts[rows, :], zt[...]), zi[rows].astype(F32) + lzi[rows], inv[rows])
         du_t[rows] = backnorm(dot(gts[:, rows], zi[...], TN), zft[rows], inv_k)
@@ -268,16 +265,20 @@
     square, head, column = (WIDTH, WIDTH), (576, WIDTH), (BLOCK, 1)
     kept = call(
         early_kernel,
-        shapes(BF16, two, two) + shapes(F32, (512, 1), two) + shapes(BF16, (576, 512))
-        + shapes(BF16, head) + shapes(F32, column) + shapes(BF16, one, one)
-        + shapes(F32, column, one) + shapes(BF16, (576, 512), one),
-        scratches(BF16, square, square, two, two, two) + scratches(F32, one)
-        + scratches(BF16, (512, 512)) + [pltpu.SemaphoreType.DMA((6,))],
-        2 * 9 * 340_000_000, "ssvvvvhh", 40 * MIB,
+        shapes(BF16, two, two) + shapes(F32, (512, 1)) + shapes(BF16, (576, 512), head, two, two)
+        + shapes(F32, (512, 1)) + shapes(BF16, (576, 512)),
+        scratches(BF16, square, square, two, two) + [pltpu.SemaphoreType.DMA((6,))],
+        2 * 6 * 340_000_000, "ssvvvvhh", 44 * MIB,
     )(core, params, img, txt, other_img, other_txt, img_head, txt_head)
 
     near, far, *kept = lax.optimization_barrier((near, far, *kept))
     near_o, far_o = swap(near), swap(far)
+    zi, zt, lzt, invt = kept[0], kept[5], kept[6], kept[7]
+    own = call(
+        own_kernel,
+        shapes(F32, column, two, one) + shapes(BF16, one), scratches(BF16, (512, 512)),
+        2 * 2 * 340_000_000, "ssvvvv", 8 * MIB,
+    )(core, params, zi, zt, lzt, invt)
     term, loss, loss_far = call(
         late_kernel,
         shapes(BF16, square) + shapes(F32, (1, BLOCK), (1, BLOCK)),
@@ -285,7 +286,7 @@
         + scratches(BF16, (512, 512), (BLOCK, BLOCK)) + scratches(F32, column, column)
         + scratches(BF16, three, (4 * BLOCK, WIDTH), (576, 512), (576, BLOCK)),
         2 * 10 * 340_000_000, "ss" + "v" * 19,
-    )(core, params, near, near_o, far, far_o, img_head, txt_head, *kept)
+    )(core, params, near, near_o, far, far_o, img_head, txt_head, *kept, *own)
 
     loss_far = lax.ppermute(loss_far, AXES, chip_shift(2))
     got = lax.all_to_all(term, AXES, 0, 0, axis_index_groups=first_groups(), tiled=True)

time: 89.9 us -> 89.5 us (level)
  waiting for transfers between devices: 14.8 us -> 13.4 us
    ppermute x4, waiting for transfers between devices: 1.78 us -> 0.01 us  [swap(): return lax.ppermute(a, AXES, core_swap())]
    pallas_call x1 -> x2, Pallas kernels: 11.7 us -> 12.3 us  [the longest x1 8.68 us: local(): call(early_kernel, shapes(BF16, two, two) + shapes(F32, (512, 1)) + shape...]
  transfers between devices with their start and end apart: 8 -> 8, of which waited for: 3 -> 2; matrix products, arithmetic and copies ran while one was open for 1% -> 1% of each run, Pallas kernels for 13% -> 14%
where the time goes in v3:
time: 89.5 us; the launch traced here: 89.1 us
  Pallas kernels  27.9 us (31%)
  blocking collectives  22.8 us (25%)
  starting transfers between devices  19.7 us (22%)
  waiting for transfers between devices  13.4 us (15%)
  local copies, waits for them, and re-layouts  2.14 us (2%)
  between operations  2.07 us (2%)
  other arithmetic  1.07 us (1%)
    all_to_all x1, blocking collectives, local(): lax.all_to_all(term, AXES, 0, 0, axis_index_groups=first_groups(), tiled=...  22.8 us
    pallas_call x1, Pallas kernels, local(): call(late_kernel, shapes(BF16, square) + shapes(F32, (1, BLOCK), (1, BLOC...  13.4 us
    pallas_call x1, Pallas kernels, local(): call(early_kernel, shapes(BF16, two, two) + shapes(F32, (512, 1)) + shape...  8.68 us
    ppermute x1, starting transfers between devices, local(): lax.ppermute(jnp.where(first, img[:128], other_img[128:]), AXES, chip_shi...  8.1 us
    all_to_all x1, waiting for transfers between devices, local(): lax.all_to_all(half, AXES, 0, 0, axis_index_groups=second_groups(), tiled...  7.79 us
    all_to_all x1, starting transfers between devices, local(): lax.all_to_all(half, AXES, 0, 0, axis_index_groups=second_groups(), tiled...  5.68 us
    ppermute x1, waiting for transfers between devices, local(): loss_far = lax.ppermute(loss_far, AXES, chip_shift(2))  5.56 us
    ppermute x4, starting transfers between devices, swap(): return lax.ppermute(a, AXES, core_swap())  4.58 us
  transfers between devices with their start and end apart: 8, of which 2 were waited for; matrix products, arithmetic and copies ran while one was open for 1% of the time, Pallas kernels for 14%

profile of v3, /device:TPU:1, one launch (start us, length us, event | category | flops | bytes accessed | tf_op | source)
XLA Modules:
  0.0 89.1 jit_solution(14808361296972662585)
XLA Ops:
  0.6 3.3 %collective-permute-start.1 = (bf16[256,1152]{1,0:T(8,128)(2,1)}, bf16[256,1152]{1,0:T(8,128)(2,1)S(1)}, u32[]{:S(2)}, u32[]{:S(2)}) collective-permute-start(bf16[256,1152]{1,0:T(8,128)(2,1)} %bitcast.15), channel_id=1, source_target_pairs={{0,2},{1,3},{2,0},{3,1},{4,6},{5,7},{6,4},{7,5},{8,10},{9,11},{10,... | collective-permute-start | bytes 1769480 | tf_op jit(solution)/shard_map/ppermute | solution.py:257
  4.0 0.1 collective-permute-start.3
  4.1 1.0 %collective-permute-start = (bf16[256,1152]{1,0:T(8,128)(2,1)}, bf16[256,1152]{1,0:T(8,128)(2,1)S(1)}, u32[]{:S(2)}, u32[]{:S(2)}) collective-permute-start(bf16[256,1152]{1,0:T(8,128)(2,1)} %bitcast.18), channel_id=1, source_target_pairs={{0,4},{1,5},{2,6},{3,7},{4,8},{5,9},{6,10},{7,11},{8,12},{9,13},{1... | collective-permute-start | bytes 1769480 | tf_op jit(solution)/shard_map/ppermute | solution.py:259
  6.4 0.1 pad_maximum_fusion.par_ref
  6.5 0.0 collective-permute-done.1.oimg
  6.5 1.0 %slice_select_fusion = bf16[128,1152]{1,0:T(8,128)(2,1)S(1)} fusion(bf16[256,1152]{1,0:T(8,128)(2,1)S(1)} %collective-permute-done.1.oimg, bf16[1,256,1152]{2,1,0:T(8,128)(2,1)} %param.6, pred[]{:T(512)S(6)} %eq.3), kind=kLoop, calls=%fused_computation | loop fusion | flops 147456 | bytes 884737 | tf_op jit(solution)/shard_map/jit(_where)/select_n | solution.py:261
  7.5 8.1 %collective-permute-start.2 = (bf16[128,1152]{1,0:T(8,128)(2,1)S(1)}, bf16[128,1152]{1,0:T(8,128)(2,1)S(1)}, u32[]{:S(2)}, u32[]{:S(2)}) collective-permute-start(bf16[128,1152]{1,0:T(8,128)(2,1)S(1)} %slice_select_fusion), channel_id=1, source_target_pairs={{0,248},{1,249},{2,250},{3,251},{4,252},{5,253},{6,254},{7,255},{8... | collective-permute-start | bytes 884744 | tf_op jit(solution)/shard_map/ppermute | solution.py:261
  15.6 0.0 collective-permute-done.3.otxt
  15.6 1.1 %copy-done = bf16[1,256,1152]{2,1,0:T(8,128)(2,1)S(1)} copy-done((bf16[1,256,1152]{2,1,0:T(8,128)(2,1)S(1)}, bf16[1,256,1152]{2,1,0:T(8,128)(2,1)}, u32[]{:S(2)}) %copy-start) | copy-done | bytes 589848
  16.7 1.1 %copy-done.3 = bf16[1,256,1152]{2,1,0:T(8,128)(2,1)S(1)} copy-done((bf16[1,256,1152]{2,1,0:T(8,128)(2,1)S(1)}, bf16[1,256,1152]{2,1,0:T(8,128)(2,1)}, u32[]{:S(2)}) %copy-start.3) | copy-done | bytes 589848
  17.7 8.7 %shard_map.77 = (bf16[512,1152]{1,0:T(8,128)(2,1)S(1)}, bf16[512,1152]{1,0:T(8,128)(2,1)S(1)}, f32[512,1]{1,0:T(8,128)S(1)}, bf16[576,512]{1,0:T(8,128)(2,1)S(1)...) custom-call(s32[1]{0:T(128)} %bitcast.core_ref, ...), custom_call_target="tpu_custom_call" | custom-call | flops 4080000000 | bytes 8388608 | tf_op jit(solution)/shard_map/pallas_call | solution.py:266
  26.4 0.0 collective-permute-done.near
  26.4 0.0 copy-start.1
  26.4 1.1 %collective-permute-start.4 = (bf16[256,1152]{1,0:T(8,128)(2,1)S(1)}, bf16[256,1152]{1,0:T(8,128)(2,1)S(1)}, u32[]{:S(2)}, u32[]{:S(2)}) collective-permute-start(bf16[256,1152]{1,0:T(8,128)(2,1)S(1)} %collective-permute-done.near), channel_id=1, source_target_pairs={{0,2},{1,3},{2,0},{3,1},{4,6},{5,7},{6,4},{7,5},{8,10},{9,11},{10,... | collective-permute-start | bytes 1769480 | tf_op jit(solution)/shard_map/ppermute | solution.py:257
  27.5 0.1 collective-permute-start.5
  27.6 3.7 %shard_map.78 = (f32[256,1]{1,0:T(8,128)S(1)}, f32[512,1152]{1,0:T(8,128)S(1)}, f32[256,1152]{1,0:T(8,128)S(1)}, bf16[256,1152]{1,0:T(8,128)(2,1)S(1)}) custom-call(s32[1]{0:T(128)} %bitcast.core_ref, f32[2]{0:T(128)S(1)} %pad_maximum_fusion.par_ref, bf16[512,1152]{1,0:T(8,128)(2,1)S(1)} %get-tuple-element.42.zi, ...), custom_call_target="tpu_custom_call" | custom-call | flops 1360000000 | bytes 8388608 | tf_op jit(solution)/shard_map/pallas_call | solution.py:277
  31.3 13.4 %shard_map.79 = (bf16[1152,1152]{1,0:T(8,128)(2,1)S(1)}, f32[1,256]{1,0:T(1,128)S(1)}, f32[1,256]{1,0:T(1,128)S(1)}) custom-call(s32[1]{0:T(128)} %bitcast.core_ref, f32[2]{0:T(128)S(1)} %pad_maximum_fusion.par_ref, bf16[256,1152]{1,0:T(8,128)(2,1)S(1)} %collective-permute-done.near, bf16[256,1152]{1,0:T(8,128)(2,1)S(1)} %collective-permute-done.4.near_o, ...), custom_call_target="tpu_custom_call" | custom-call | flops 6800000000 | bytes 8388608 | tf_op jit(solution)/shard_map/pallas_call | solution.py:282
  44.7 22.8 %all_to_all.22 = bf16[8,144,1152]{2,1,0:T(8,128)(2,1)S(1)} all-to-all(bf16[8,144,1152]{2,1,0:T(8,128)(2,1)S(1)} %bitcast.13), channel_id=1, replica_groups={{0,1,4,5,32,33,36,37},{2,10,18,26,226,234,242,250},{3,11,19,27,227,235,..., dimensions={0} | all-to-all | bytes 5308416 | tf_op jit(solution)/shard_map/all_to_all | solution.py:292
  67.5 1.5 %shard_map.80 = bf16[1408,128]{1,0:T(8,128)(2,1)} custom-call(bf16[1152,1152]{1,0:T(8,128)(2,1)S(1)} %bitcast.12), custom_call_target="tpu_custom_call" | custom-call | flops 10000000 | bytes 8388608 | tf_op jit(solution)/shard_map/pallas_call | solution.py:293
  69.0 5.7 %all-to-all-start.1 = ((bf16[16,88,128]{2,1,0:T(8,128)(2,1)}), bf16[16,88,128]{2,1,0:T(8,128)(2,1)S(1)}, u32[]{:S(2)}, u32[]{:S(2)}) async-start(bf16[16,88,128]{2,1,0:T(8,128)(2,1)} %bitcast.8), calls=%async_computation.1 | async-start | bytes 720896 | tf_op jit(solution)/shard_map/all_to_all | solution.py:296
  74.7 0.4 collective-permute-start.6
  75.1 5.6 %collective-permute-done.6.loss_far = f32[1,256]{1,0:T(1,128)S(1)} collective-permute-done((f32[1,256]{1,0:T(1,128)S(1)}, f32[1,256]{1,0:T(1,128)S(1)}, u32[]{:S(2)}, u32[]{:S(2)}) %collective-permute-start.6) | collective-permute-done | bytes 1056 | tf_op jit(solution)/shard_map/ppermute | solution.py:291
  80.6 7.8 %all-to-all-done.1 = bf16[16,88,128]{2,1,0:T(8,128)(2,1)S(1)} async-done(((bf16[16,88,128]{2,1,0:T(8,128)(2,1)}), bf16[16,88,128]{2,1,0:T(8,128)(2,1)S(1)}, u32[]{:S(2)}, u32[]{:S(2)}) %all-to-all-start.1) | async-done | bytes 360480 | tf_op jit(solution)/shard_map/all_to_all | solution.py:296
  88.4 0.7 shard_map.81
  (8 shorter events, 0.0 us)
Async XLA Ops:
  0.6 5.9 %collective-permute-start.1 = (bf16[256,1152]{1,0:T(8,128)(2,1)}, bf16[256,1152]{1,0:T(8,128)(2,1)S(1)}, u32[]{:S(2)}, u32[]{:S(2)}) collective-permute-start(bf16[256,1152]{1,0:T(8,128)(2,1)} %bitcast.15), channel_id=1, source_target_pairs={{0,2},{1,3},{2,0},{3,1},{4,6},{5,7},{6,4},{7,5},{8,10},{9,11},{10,... | collective-permute-start | bytes 1769480 | tf_op jit(solution)/shard_map/ppermute | solution.py:257
  4.0 11.6 %collective-permute-start.3 = (bf16[256,1152]{1,0:T(8,128)(2,1)}, bf16[256,1152]{1,0:T(8,128)(2,1)S(1)}, u32[]{:S(2)}, u32[]{:S(2)}) collective-permute-start(bf16[256,1152]{1,0:T(8,128)(2,1)} %bitcast.17), channel_id=1, source_target_pairs={{0,2},{1,3},{2,0},{3,1},{4,6},{5,7},{6,4},{7,5},{8,10},{9,11},{10,... | collective-permute-start | bytes 1769480 | tf_op jit(solution)/shard_map/ppermute | solution.py:257
  4.1 22.4 %collective-permute-start = (bf16[256,1152]{1,0:T(8,128)(2,1)}, bf16[256,1152]{1,0:T(8,128)(2,1)S(1)}, u32[]{:S(2)}, u32[]{:S(2)}) collective-permute-start(bf16[256,1152]{1,0:T(8,128)(2,1)} %bitcast.18), channel_id=1, source_target_pairs={{0,4},{1,5},{2,6},{3,7},{4,8},{5,9},{6,10},{7,11},{8,12},{9,13},{1... | collective-permute-start | bytes 1769480 | tf_op jit(solution)/shard_map/ppermute | solution.py:259
  7.5 18.9 %collective-permute-start.2 = (bf16[128,1152]{1,0:T(8,128)(2,1)S(1)}, bf16[128,1152]{1,0:T(8,128)(2,1)S(1)}, u32[]{:S(2)}, u32[]{:S(2)}) collective-permute-start(bf16[128,1152]{1,0:T(8,128)(2,1)S(1)} %slice_select_fusion), channel_id=1, source_target_pairs={{0,248},{1,249},{2,250},{3,251},{4,252},{5,253},{6,254},{7,255},{8... | collective-permute-start | bytes 884744 | tf_op jit(solution)/shard_map/ppermute | solution.py:261
  15.6 1.1 %copy-start = (bf16[1,256,1152]{2,1,0:T(8,128)(2,1)S(1)}, bf16[1,256,1152]{2,1,0:T(8,128)(2,1)}, u32[]{:S(2)}) copy-start(bf16[1,256,1152]{2,1,0:T(8,128)(2,1)} %param.6) | copy-start | bytes 1769476
  16.7 1.1 %copy-start.3 = (bf16[1,256,1152]{2,1,0:T(8,128)(2,1)S(1)}, bf16[1,256,1152]{2,1,0:T(8,128)(2,1)}, u32[]{:S(2)}) copy-start(bf16[1,256,1152]{2,1,0:T(8,128)(2,1)} %param.7) | copy-start | bytes 1769476
  17.7 13.6 %copy-start.2 = (bf16[1152,1152]{1,0:T(8,128)(2,1)S(1)}, bf16[1152,1152]{1,0:T(8,128)(2,1)}, u32[]{:S(2)}) copy-start(bf16[1152,1152]{1,0:T(8,128)(2,1)} %htxt.1) | copy-start | bytes 7962628
  26.4 4.9 %copy-start.1 = (bf16[1152,1152]{1,0:T(8,128)(2,1)S(1)}, bf16[1152,1152]{1,0:T(8,128)(2,1)}, u32[]{:S(2)}) copy-start(bf16[1152,1152]{1,0:T(8,128)(2,1)} %himg.1) | copy-start | bytes 7962628
  26.4 4.8 %collective-permute-start.4 = (bf16[256,1152]{1,0:T(8,128)(2,1)S(1)}, bf16[256,1152]{1,0:T(8,128)(2,1)S(1)}, u32[]{:S(2)}, u32[]{:S(2)}) collective-permute-start(bf16[256,1152]{1,0:T(8,128)(2,1)S(1)} %collective-permute-done.near), channel_id=1, source_target_pairs={{0,2},{1,3},{2,0},{3,1},{4,6},{5,7},{6,4},{7,5},{8,10},{9,11},{10,... | collective-permute-start | bytes 1769480 | tf_op jit(solution)/shard_map/ppermute | solution.py:257
  27.5 3.8 %collective-permute-start.5 = (bf16[128,1152]{1,0:T(8,128)(2,1)S(1)}, bf16[128,1152]{1,0:T(8,128)(2,1)S(1)}, u32[]{:S(2)}, u32[]{:S(2)}) collective-permute-start(bf16[128,1152]{1,0:T(8,128)(2,1)S(1)} %collective-permute-done.2.far), channel_id=1, source_target_pairs={{0,2},{1,3},{2,0},{3,1},{4,6},{5,7},{6,4},{7,5},{8,10},{9,11},{10,... | collective-permute-start | bytes 884744 | tf_op jit(solution)/shard_map/ppermute | solution.py:257
  69.0 19.4 %all-to-all-start.1 = ((bf16[16,88,128]{2,1,0:T(8,128)(2,1)}), bf16[16,88,128]{2,1,0:T(8,128)(2,1)S(1)}, u32[]{:S(2)}, u32[]{:S(2)}) async-start(bf16[16,88,128]{2,1,0:T(8,128)(2,1)} %bitcast.8), calls=%async_computation.1 | async-start | bytes 720896 | tf_op jit(solution)/shard_map/all_to_all | solution.py:296
  74.7 5.9 %collective-permute-start.6 = (f32[1,256]{1,0:T(1,128)S(1)}, f32[1,256]{1,0:T(1,128)S(1)}, u32[]{:S(2)}, u32[]{:S(2)}) collective-permute-start(f32[1,256]{1,0:T(1,128)S(1)} %get-tuple-element.57), channel_id=1, source_target_pairs={{0,8},{1,9},{2,10},{3,11},{4,12},{5,13},{6,14},{7,15},{8,16},{9,17... | collective-permute-start | bytes 3080 | tf_op jit(solution)/shard_map/ppermute | solution.py:291

commit v4 on v3

--- a/solution.py
+++ b/solution.py
@@ -171,12 +171,9 @@
     zf, inv2 = normalise(f2[...], himg[...])
     zf2[...] = zf
     z2[...] = zf.astype(BF16)
-    inv_t = []
-    for rows in (lo, hi):
-        zf, i = normalise(ft[rows], htxt[...])
-        zft[rows] = zf
-        zt[rows] = zf.astype(BF16)
-        inv_t.append(i)
+    zf, inv_t = normalise(ft[...], htxt[...])
+    zft[...] = zf
+    zt[...] = zf.astype(BF16)
     ft2[...] = dot(pick[...], f2[...], NT).astype(BF16)
     ftt[...] = dot(pick[...], ft[...], NT).astype(BF16)
     loss[...] = loss_near[...]
@@ -189,9 +186,9 @@
     du_i[end] = backnorm(dot(gt2[...], zown[HI]), zf2[...], inv2)
     du_t[2 * BLOCK : 3 * BLOCK] = du3[...]
     du_t[3 * BLOCK :] = backnorm(g4[...] + dot(gt2[...], z2[...], TN), zown[HI].astype(F32) + lzown[HI], invown[HI])
-    for rows, inv_k in zip((lo, hi), inv_t):
-        du_i[rows] = backnorm(dq[rows] + dot(gts[rows, :], zt[...]), zi[rows].astype(F32) + lzi[rows], inv[rows])
-        du_t[rows] = backnorm(dot(gts[:, rows], zi[...], TN), zft[rows], inv_k)
+    pair = slice(0, 2 * BLOCK)
+    du_i[pair] = backnorm(dq[...] + dot(gts[...], zt[...]), zi[...].astype(F32) + lzi[...], inv[...])
+    du_t[pair] = backnorm(dot(gts[...], zi[...], TN), zft[...], inv_t)
     for first in range(0, WIDTH, 256):
         cols = slice(first, min(first + 256, WIDTH))
         g_i = dot(fti[...], du_i[: 2 * BLOCK, cols]) + dot(ft2[...], du_i[end, cols])

time: 89.5 us -> 89 us (level)
  no operation moved by 1% of the time
where the time goes in v4:
time: 89 us; the launch traced here: 88.6 us
  Pallas kernels  27.4 us (31%)
  blocking collectives  22.8 us (26%)
  starting transfers between devices  19.7 us (22%)
  waiting for transfers between devices  13.4 us (15%)
  local copies, waits for them, and re-layouts  2.14 us (2%)
  between operations  2.07 us (2%)
  other arithmetic  1.07 us (1%)
    all_to_all x1, blocking collectives, local(): lax.all_to_all(term, AXES, 0, 0, axis_index_groups=first_groups(), tiled=...  22.8 us
    pallas_call x1, Pallas kernels, local(): call(late_kernel, shapes(BF16, square) + shapes(F32, (1, BLOCK), (1, BLOC...  12.9 us
    pallas_call x1, Pallas kernels, local(): call(early_kernel, shapes(BF16, two, two) + shapes(F32, (512, 1)) + shape...  8.68 us
    ppermute x1, starting transfers between devices, local(): lax.ppermute(jnp.where(first, img[:128], other_img[128:]), AXES, chip_shi...  8.1 us
    all_to_all x1, waiting for transfers between devices, local(): lax.all_to_all(half, AXES, 0, 0, axis_index_groups=second_groups(), tiled...  7.79 us
    all_to_all x1, starting transfers between devices, local(): lax.all_to_all(half, AXES, 0, 0, axis_index_groups=second_groups(), tiled...  5.69 us
    ppermute x1, waiting for transfers between devices, local(): loss_far = lax.ppermute(loss_far, AXES, chip_shift(2))  5.56 us
    ppermute x4, starting transfers between devices, swap(): return lax.ppermute(a, AXES, core_swap())  4.58 us
  transfers between devices with their start and end apart: 8, of which 2 were waited for; matrix products, arithmetic and copies ran while one was open for 1% of the time, Pallas kernels for 14%

profile of v4, /device:TPU:1, one launch (start us, length us, event | category | flops | bytes accessed | tf_op | source)
XLA Modules:
  0.0 88.6 jit_solution(8674001789066830778)
XLA Ops:
  0.6 3.3 %collective-permute-start.1 = (bf16[256,1152]{1,0:T(8,128)(2,1)}, bf16[256,1152]{1,0:T(8,128)(2,1)S(1)}, u32[]{:S(2)}, u32[]{:S(2)}) collective-permute-start(bf16[256,1152]{1,0:T(8,128)(2,1)} %bitcast.15), channel_id=1, source_target_pairs={{0,2},{1,3},{2,0},{3,1},{4,6},{5,7},{6,4},{7,5},{8,10},{9,11},{10,... | collective-permute-start | bytes 1769480 | tf_op jit(solution)/shard_map/ppermute | solution.py:254
  4.0 0.1 collective-permute-start.3
  4.1 1.0 %collective-permute-start = (bf16[256,1152]{1,0:T(8,128)(2,1)}, bf16[256,1152]{1,0:T(8,128)(2,1)S(1)}, u32[]{:S(2)}, u32[]{:S(2)}) collective-permute-start(bf16[256,1152]{1,0:T(8,128)(2,1)} %bitcast.18), channel_id=1, source_target_pairs={{0,4},{1,5},{2,6},{3,7},{4,8},{5,9},{6,10},{7,11},{8,12},{9,13},{1... | collective-permute-start | bytes 1769480 | tf_op jit(solution)/shard_map/ppermute | solution.py:256
  6.4 0.1 pad_maximum_fusion.par_ref
  6.5 0.0 collective-permute-done.1.oimg
  6.5 1.0 %slice_select_fusion = bf16[128,1152]{1,0:T(8,128)(2,1)S(1)} fusion(bf16[256,1152]{1,0:T(8,128)(2,1)S(1)} %collective-permute-done.1.oimg, bf16[1,256,1152]{2,1,0:T(8,128)(2,1)} %param.6, pred[]{:T(512)S(6)} %eq.3), kind=kLoop, calls=%fused_computation | loop fusion | flops 147456 | bytes 884737 | tf_op jit(solution)/shard_map/jit(_where)/select_n | solution.py:258
  7.5 8.1 %collective-permute-start.2 = (bf16[128,1152]{1,0:T(8,128)(2,1)S(1)}, bf16[128,1152]{1,0:T(8,128)(2,1)S(1)}, u32[]{:S(2)}, u32[]{:S(2)}) collective-permute-start(bf16[128,1152]{1,0:T(8,128)(2,1)S(1)} %slice_select_fusion), channel_id=1, source_target_pairs={{0,248},{1,249},{2,250},{3,251},{4,252},{5,253},{6,254},{7,255},{8... | collective-permute-start | bytes 884744 | tf_op jit(solution)/shard_map/ppermute | solution.py:258
  15.6 0.0 collective-permute-done.3.otxt
  15.6 1.1 %copy-done = bf16[1,256,1152]{2,1,0:T(8,128)(2,1)S(1)} copy-done((bf16[1,256,1152]{2,1,0:T(8,128)(2,1)S(1)}, bf16[1,256,1152]{2,1,0:T(8,128)(2,1)}, u32[]{:S(2)}) %copy-start) | copy-done | bytes 589848
  16.7 1.1 %copy-done.3 = bf16[1,256,1152]{2,1,0:T(8,128)(2,1)S(1)} copy-done((bf16[1,256,1152]{2,1,0:T(8,128)(2,1)S(1)}, bf16[1,256,1152]{2,1,0:T(8,128)(2,1)}, u32[]{:S(2)}) %copy-start.3) | copy-done | bytes 589848
  17.7 8.7 %shard_map.77 = (bf16[512,1152]{1,0:T(8,128)(2,1)S(1)}, bf16[512,1152]{1,0:T(8,128)(2,1)S(1)}, f32[512,1]{1,0:T(8,128)S(1)}, bf16[576,512]{1,0:T(8,128)(2,1)S(1)...) custom-call(s32[1]{0:T(128)} %bitcast.core_ref, ...), custom_call_target="tpu_custom_call" | custom-call | flops 4080000000 | bytes 8388608 | tf_op jit(solution)/shard_map/pallas_call | solution.py:263
  26.4 0.0 collective-permute-done.near
  26.4 0.0 copy-start.1
  26.4 1.1 %collective-permute-start.4 = (bf16[256,1152]{1,0:T(8,128)(2,1)S(1)}, bf16[256,1152]{1,0:T(8,128)(2,1)S(1)}, u32[]{:S(2)}, u32[]{:S(2)}) collective-permute-start(bf16[256,1152]{1,0:T(8,128)(2,1)S(1)} %collective-permute-done.near), channel_id=1, source_target_pairs={{0,2},{1,3},{2,0},{3,1},{4,6},{5,7},{6,4},{7,5},{8,10},{9,11},{10,... | collective-permute-start | bytes 1769480 | tf_op jit(solution)/shard_map/ppermute | solution.py:254
  27.5 0.1 collective-permute-start.5
  27.6 3.7 %shard_map.78 = (f32[256,1]{1,0:T(8,128)S(1)}, f32[512,1152]{1,0:T(8,128)S(1)}, f32[256,1152]{1,0:T(8,128)S(1)}, bf16[256,1152]{1,0:T(8,128)(2,1)S(1)}) custom-call(s32[1]{0:T(128)} %bitcast.core_ref, f32[2]{0:T(128)S(1)} %pad_maximum_fusion.par_ref, bf16[512,1152]{1,0:T(8,128)(2,1)S(1)} %get-tuple-element.42.zi, ...), custom_call_target="tpu_custom_call" | custom-call | flops 1360000000 | bytes 8388608 | tf_op jit(solution)/shard_map/pallas_call | solution.py:274
  31.3 12.9 %shard_map.79 = (bf16[1152,1152]{1,0:T(8,128)(2,1)S(1)}, f32[1,256]{1,0:T(1,128)S(1)}, f32[1,256]{1,0:T(1,128)S(1)}) custom-call(s32[1]{0:T(128)} %bitcast.core_ref, f32[2]{0:T(128)S(1)} %pad_maximum_fusion.par_ref, bf16[256,1152]{1,0:T(8,128)(2,1)S(1)} %collective-permute-done.near, bf16[256,1152]{1,0:T(8,128)(2,1)S(1)} %collective-permute-done.4.near_o, ...), custom_call_target="tpu_custom_call" | custom-call | flops 6800000000 | bytes 8388608 | tf_op jit(solution)/shard_map/pallas_call | solution.py:279
  44.2 22.8 %all_to_all.22 = bf16[8,144,1152]{2,1,0:T(8,128)(2,1)S(1)} all-to-all(bf16[8,144,1152]{2,1,0:T(8,128)(2,1)S(1)} %bitcast.13), channel_id=1, replica_groups={{0,1,4,5,32,33,36,37},{2,10,18,26,226,234,242,250},{3,11,19,27,227,235,..., dimensions={0} | all-to-all | bytes 5308416 | tf_op jit(solution)/shard_map/all_to_all | solution.py:289
  67.0 1.5 %shard_map.80 = bf16[1408,128]{1,0:T(8,128)(2,1)} custom-call(bf16[1152,1152]{1,0:T(8,128)(2,1)S(1)} %bitcast.12), custom_call_target="tpu_custom_call" | custom-call | flops 10000000 | bytes 8388608 | tf_op jit(solution)/shard_map/pallas_call | solution.py:290
  68.5 5.7 %all-to-all-start.1 = ((bf16[16,88,128]{2,1,0:T(8,128)(2,1)}), bf16[16,88,128]{2,1,0:T(8,128)(2,1)S(1)}, u32[]{:S(2)}, u32[]{:S(2)}) async-start(bf16[16,88,128]{2,1,0:T(8,128)(2,1)} %bitcast.8), calls=%async_computation.1 | async-start | bytes 720896 | tf_op jit(solution)/shard_map/all_to_all | solution.py:293
  74.2 0.4 collective-permute-start.6
  74.6 5.6 %collective-permute-done.6.loss_far = f32[1,256]{1,0:T(1,128)S(1)} collective-permute-done((f32[1,256]{1,0:T(1,128)S(1)}, f32[1,256]{1,0:T(1,128)S(1)}, u32[]{:S(2)}, u32[]{:S(2)}) %collective-permute-start.6) | collective-permute-done | bytes 1056 | tf_op jit(solution)/shard_map/ppermute | solution.py:288
  80.1 7.8 %all-to-all-done.1 = bf16[16,88,128]{2,1,0:T(8,128)(2,1)S(1)} async-done(((bf16[16,88,128]{2,1,0:T(8,128)(2,1)}), bf16[16,88,128]{2,1,0:T(8,128)(2,1)S(1)}, u32[]{:S(2)}, u32[]{:S(2)}) %all-to-all-start.1) | async-done | bytes 360480 | tf_op jit(solution)/shard_map/all_to_all | solution.py:293
  87.9 0.7 shard_map.81
  (8 shorter events, 0.0 us)
Async XLA Ops:
  0.6 5.9 %collective-permute-start.1 = (bf16[256,1152]{1,0:T(8,128)(2,1)}, bf16[256,1152]{1,0:T(8,128)(2,1)S(1)}, u32[]{:S(2)}, u32[]{:S(2)}) collective-permute-start(bf16[256,1152]{1,0:T(8,128)(2,1)} %bitcast.15), channel_id=1, source_target_pairs={{0,2},{1,3},{2,0},{3,1},{4,6},{5,7},{6,4},{7,5},{8,10},{9,11},{10,... | collective-permute-start | bytes 1769480 | tf_op jit(solution)/shard_map/ppermute | solution.py:254
  4.0 11.6 %collective-permute-start.3 = (bf16[256,1152]{1,0:T(8,128)(2,1)}, bf16[256,1152]{1,0:T(8,128)(2,1)S(1)}, u32[]{:S(2)}, u32[]{:S(2)}) collective-permute-start(bf16[256,1152]{1,0:T(8,128)(2,1)} %bitcast.17), channel_id=1, source_target_pairs={{0,2},{1,3},{2,0},{3,1},{4,6},{5,7},{6,4},{7,5},{8,10},{9,11},{10,... | collective-permute-start | bytes 1769480 | tf_op jit(solution)/shard_map/ppermute | solution.py:254
  4.1 22.4 %collective-permute-start = (bf16[256,1152]{1,0:T(8,128)(2,1)}, bf16[256,1152]{1,0:T(8,128)(2,1)S(1)}, u32[]{:S(2)}, u32[]{:S(2)}) collective-permute-start(bf16[256,1152]{1,0:T(8,128)(2,1)} %bitcast.18), channel_id=1, source_target_pairs={{0,4},{1,5},{2,6},{3,7},{4,8},{5,9},{6,10},{7,11},{8,12},{9,13},{1... | collective-permute-start | bytes 1769480 | tf_op jit(solution)/shard_map/ppermute | solution.py:256
  7.5 18.9 %collective-permute-start.2 = (bf16[128,1152]{1,0:T(8,128)(2,1)S(1)}, bf16[128,1152]{1,0:T(8,128)(2,1)S(1)}, u32[]{:S(2)}, u32[]{:S(2)}) collective-permute-start(bf16[128,1152]{1,0:T(8,128)(2,1)S(1)} %slice_select_fusion), channel_id=1, source_target_pairs={{0,248},{1,249},{2,250},{3,251},{4,252},{5,253},{6,254},{7,255},{8... | collective-permute-start | bytes 884744 | tf_op jit(solution)/shard_map/ppermute | solution.py:258
  15.6 1.1 %copy-start = (bf16[1,256,1152]{2,1,0:T(8,128)(2,1)S(1)}, bf16[1,256,1152]{2,1,0:T(8,128)(2,1)}, u32[]{:S(2)}) copy-start(bf16[1,256,1152]{2,1,0:T(8,128)(2,1)} %param.6) | copy-start | bytes 1769476
  16.7 1.1 %copy-start.3 = (bf16[1,256,1152]{2,1,0:T(8,128)(2,1)S(1)}, bf16[1,256,1152]{2,1,0:T(8,128)(2,1)}, u32[]{:S(2)}) copy-start(bf16[1,256,1152]{2,1,0:T(8,128)(2,1)} %param.7) | copy-start | bytes 1769476
  17.7 13.6 %copy-start.2 = (bf16[1152,1152]{1,0:T(8,128)(2,1)S(1)}, bf16[1152,1152]{1,0:T(8,128)(2,1)}, u32[]{:S(2)}) copy-start(bf16[1152,1152]{1,0:T(8,128)(2,1)} %htxt.1) | copy-start | bytes 7962628
  26.4 4.9 %copy-start.1 = (bf16[1152,1152]{1,0:T(8,128)(2,1)S(1)}, bf16[1152,1152]{1,0:T(8,128)(2,1)}, u32[]{:S(2)}) copy-start(bf16[1152,1152]{1,0:T(8,128)(2,1)} %himg.1) | copy-start | bytes 7962628
  26.4 4.8 %collective-permute-start.4 = (bf16[256,1152]{1,0:T(8,128)(2,1)S(1)}, bf16[256,1152]{1,0:T(8,128)(2,1)S(1)}, u32[]{:S(2)}, u32[]{:S(2)}) collective-permute-start(bf16[256,1152]{1,0:T(8,128)(2,1)S(1)} %collective-permute-done.near), channel_id=1, source_target_pairs={{0,2},{1,3},{2,0},{3,1},{4,6},{5,7},{6,4},{7,5},{8,10},{9,11},{10,... | collective-permute-start | bytes 1769480 | tf_op jit(solution)/shard_map/ppermute | solution.py:254
  27.5 3.8 %collective-permute-start.5 = (bf16[128,1152]{1,0:T(8,128)(2,1)S(1)}, bf16[128,1152]{1,0:T(8,128)(2,1)S(1)}, u32[]{:S(2)}, u32[]{:S(2)}) collective-permute-start(bf16[128,1152]{1,0:T(8,128)(2,1)S(1)} %collective-permute-done.2.far), channel_id=1, source_target_pairs={{0,2},{1,3},{2,0},{3,1},{4,6},{5,7},{6,4},{7,5},{8,10},{9,11},{10,... | collective-permute-start | bytes 884744 | tf_op jit(solution)/shard_map/ppermute | solution.py:254
  68.5 19.4 %all-to-all-start.1 = ((bf16[16,88,128]{2,1,0:T(8,128)(2,1)}), bf16[16,88,128]{2,1,0:T(8,128)(2,1)S(1)}, u32[]{:S(2)}, u32[]{:S(2)}) async-start(bf16[16,88,128]{2,1,0:T(8,128)(2,1)} %bitcast.8), calls=%async_computation.1 | async-start | bytes 720896 | tf_op jit(solution)/shard_map/all_to_all | solution.py:293
  74.2 5.9 %collective-permute-start.6 = (f32[1,256]{1,0:T(1,128)S(1)}, f32[1,256]{1,0:T(1,128)S(1)}, u32[]{:S(2)}, u32[]{:S(2)}) collective-permute-start(f32[1,256]{1,0:T(1,128)S(1)} %get-tuple-element.57), channel_id=1, source_target_pairs={{0,8},{1,9},{2,10},{3,11},{4,12},{5,13},{6,14},{7,15},{8,16},{9,17... | collective-permute-start | bytes 3080 | tf_op jit(solution)/shard_map/ppermute | solution.py:288

commit v5 on v4

--- a/solution.py
+++ b/solution.py
@@ -93,22 +93,23 @@
     return (inv * (grad - zfull * jnp.sum(grad * zfull, axis=-1, keepdims=True))).astype(BF16)
 
 
-def score(query, keys, scale, bias, diagonal, gt_ref, loss_ref, wanted):
+def score(query, keys, scale, bias, diagonal, gt_ref, kept):
     logits = scale * dot(query, keys, NT) + bias
     if diagonal is not None:
         row = lax.broadcasted_iota(jnp.int32, logits.shape, 0)
         col = lax.broadcasted_iota(jnp.int32, logits.shape, 1)
         own = col == row + diagonal
         logits = jnp.where(own, -logits, logits)
+    kept[...] = logits
     e = jnp.exp(-jnp.abs(logits))
     sig = jnp.where(logits >= 0, 1.0, e) / (1.0 + e)
     if diagonal is not None:
         sig = jnp.where(own, -sig, sig)
     gt_ref[...] = (scale * sig / BLOCK).astype(BF16)
 
-    @pl.when(wanted)
-    def _():
-        loss_ref[...] += jnp.sum(jnp.maximum(logits, 0.0) + jnp.log1p(e), axis=1, keepdims=True)
+
+def softplus_rows(x):
+    return jnp.sum(jnp.maximum(x, 0.0) + jnp.log1p(jnp.exp(-jnp.abs(x))), axis=1, keepdims=True)
 
 
 LO, HI, END = (slice(k * BLOCK, (k + 1) * BLOCK) for k in range(3))
@@ -137,18 +138,18 @@
         for copy in waits:
             copy.wait()
         ft[...] = dot(pick[...], f[...], NT).astype(BF16)
-        for rows in (LO, HI):
-            zf, i[rows] = normalise(f[rows], head[...])
-            lz[rows] = rest(zf)
-            z[rows] = zf.astype(BF16)
-
-
-def own_kernel(core_ref, par_ref, zi, zt, lzt, invt, loss, dq, g4, du3, gts):
+        zf, i[...] = normalise(f[...], head[...])
+        lz[...] = rest(zf)
+        z[...] = zf.astype(BF16)
+
+
+def own_kernel(core_ref, par_ref, zi, zt, lzt, invt, loss, dq, g4, du3, gts, kept):
     c = core_ref[0]
     scale, bias = par_ref[0], par_ref[1]
-    loss[...] = jnp.zeros_like(loss)
-    score(zi[LO], zt[LO], scale, bias, 0, gts.at[LO, LO], loss, c == 0)
-    score(zi[HI], zt[...], scale, bias, BLOCK, gts.at[HI, :], loss, c == 1)
+    kept[LO, HI] = jnp.full((BLOCK, BLOCK), -1e30, F32)
+    score(zi[LO], zt[LO], scale, bias, 0, gts.at[LO, LO], kept.at[LO, LO])
+    score(zi[HI], zt[...], scale, bias, BLOCK, gts.at[HI, :], kept.at[HI, :])
+    loss[...] = softplus_rows(kept[pl.ds(pl.multiple_of(c * BLOCK, BLOCK), BLOCK)])
     dq[LO] = dot(gts[LO, LO], zt[LO])
     dq[HI] = dot(gts[HI, :], zt[...])
     du3[...] = backnorm(dot(gts[:, LO], zi[...], TN), zt[LO].astype(F32) + lzt[LO], invt[LO])
@@ -159,7 +160,7 @@
     core_ref, par_ref, near, near_o, far, far_o,
     himg, htxt, zi, lzi, inv, fti, pick, zown, lzown, invown, ft34, loss_near, dq, g4, du3,
     out, loss_out, loss_far,
-    ft, f2, zt, zft, z2, zf2, gts, gt2, loss, loss2, du_i, du_t, ftt, ft2,
+    ft, f2, zt, zft, z2, zf2, gts, gt2, kept, kept2, du_i, du_t, ftt, ft2,
 ):
     c = core_ref[0]
     f2[pl.ds(pl.multiple_of(c * 128, 128), 128)] = far[...]
@@ -167,7 +168,7 @@
     ft[pl.ds(pl.multiple_of(c * BLOCK, BLOCK), BLOCK)] = near[...]
     ft[pl.ds(pl.multiple_of((1 - c) * BLOCK, BLOCK), BLOCK)] = near_o[...]
     scale, bias = par_ref[0], par_ref[1]
-    lo, hi, end = slice(0, BLOCK), slice(BLOCK, 2 * BLOCK), slice(2 * BLOCK, 3 * BLOCK)
+    end = END
     zf, inv2 = normalise(f2[...], himg[...])
     zf2[...] = zf
     z2[...] = zf.astype(BF16)
@@ -176,13 +177,11 @@
     zt[...] = zf.astype(BF16)
     ft2[...] = dot(pick[...], f2[...], NT).astype(BF16)
     ftt[...] = dot(pick[...], ft[...], NT).astype(BF16)
-    loss[...] = loss_near[...]
-    loss2[...] = jnp.zeros_like(loss2)
-    score(z2[...], zown[HI], scale, bias, None, gt2, loss2, c == 0)
-    score(zi[lo], zt[...], scale, bias, None, gts.at[lo, :], loss, c == 0)
-    score(zi[hi], zt[...], scale, bias, None, gts.at[hi, :], loss, c == 1)
-    loss_out[...] = jnp.transpose(jnp.broadcast_to(loss[...], (BLOCK, 128)))[:1]
-    loss_far[...] = jnp.transpose(jnp.broadcast_to(loss2[...], (BLOCK, 128)))[:1]
+    score(z2[...], zown[HI], scale, bias, None, gt2, kept2)
+    score(zi[...], zt[...], scale, bias, None, gts, kept)
+    loss = loss_near[...] + softplus_rows(kept[pl.ds(pl.multiple_of(c * BLOCK, BLOCK), BLOCK)])
+    loss_out[...] = jnp.transpose(jnp.broadcast_to(loss, (BLOCK, 128)))[:1]
+    loss_far[...] = jnp.transpose(jnp.broadcast_to(softplus_rows(kept2[...]), (BLOCK, 128)))[:1]
     du_i[end] = backnorm(dot(gt2[...], zown[HI]), zf2[...], inv2)
     du_t[2 * BLOCK : 3 * BLOCK] = du3[...]
     du_t[3 * BLOCK :] = backnorm(g4[...] + dot(gt2[...], z2[...], TN), zown[HI].astype(F32) + lzown[HI], invown[HI])
@@ -273,14 +272,14 @@
     zi, zt, lzt, invt = kept[0], kept[5], kept[6], kept[7]
     own = call(
         own_kernel,
-        shapes(F32, column, two, one) + shapes(BF16, one), scratches(BF16, (512, 512)),
-        2 * 2 * 340_000_000, "ssvvvv", 8 * MIB,
+        shapes(F32, column, two, one) + shapes(BF16, one), scratches(BF16, (512, 512)) + scratches(F32, (512, 512)),
+        2 * 2 * 340_000_000, "ssvvvv", 12 * MIB,
     )(core, params, zi, zt, lzt, invt)
     term, loss, loss_far = call(
         late_kernel,
         shapes(BF16, square) + shapes(F32, (1, BLOCK), (1, BLOCK)),
         scratches(BF16, two, one, two) + scratches(F32, two) + scratches(BF16, one) + scratches(F32, one)
-        + scratches(BF16, (512, 512), (BLOCK, BLOCK)) + scratches(F32, column, column)
+        + scratches(BF16, (512, 512), (BLOCK, BLOCK)) + scratches(F32, (512, 512), (BLOCK, BLOCK))
         + scratches(BF16, three, (4 * BLOCK, WIDTH), (576, 512), (576, BLOCK)),
         2 * 10 * 340_000_000, "ss" + "v" * 19,
     )(core, params, near, near_o, far, far_o, img_head, txt_head, *kept, *own)

time: 89 us -> 86.5 us (0.972)
  Pallas kernels: 27.4 us -> 25.4 us
    pallas_call x1, Pallas kernels: 12.9 us -> 11.5 us  [local(): call(late_kernel, shapes(BF16, square) + shapes(F32, (1, BLOCK), (1, BLOC...]
    pallas_call x1, Pallas kernels: 3.66 us -> 2.64 us  [local(): call(own_kernel, shapes(F32, column, two, one) + shapes(BF16, one), scrat...]
where the time goes in v5:
time: 86.5 us; the launch traced here: 86.1 us
  Pallas kernels  25.4 us (29%)
  blocking collectives  22.8 us (26%)
  starting transfers between devices  19.6 us (23%)
  waiting for transfers between devices  13.1 us (15%)
  local copies, waits for them, and re-layouts  2.14 us (2%)
  between operations  2.07 us (2%)
  other arithmetic  1.07 us (1%)
    all_to_all x1, blocking collectives, local(): lax.all_to_all(term, AXES, 0, 0, axis_index_groups=first_groups(), tiled=...  22.8 us
    pallas_call x1, Pallas kernels, local(): call(late_kernel, shapes(BF16, square) + shapes(F32, (1, BLOCK), (1, BLOC...  11.5 us
    pallas_call x1, Pallas kernels, local(): call(early_kernel, shapes(BF16, two, two) + shapes(F32, (512, 1)) + shape...  9.08 us
    ppermute x1, starting transfers between devices, local(): lax.ppermute(jnp.where(first, img[:128], other_img[128:]), AXES, chip_shi...  8.1 us
    all_to_all x1, waiting for transfers between devices, local(): lax.all_to_all(half, AXES, 0, 0, axis_index_groups=second_groups(), tiled...  7.49 us
    ppermute x1, waiting for transfers between devices, local(): loss_far = lax.ppermute(loss_far, AXES, chip_shift(2))  5.56 us
    all_to_all x1, starting transfers between devices, local(): lax.all_to_all(half, AXES, 0, 0, axis_index_groups=second_groups(), tiled...  5.35 us
    ppermute x4, starting transfers between devices, swap(): return lax.ppermute(a, AXES, core_swap())  4.77 us
  transfers between devices with their start and end apart: 8, of which 2 were waited for; matrix products, arithmetic and copies ran while one was open for 1% of the time, Pallas kernels for 14%

profile of v5, /device:TPU:1, one launch (start us, length us, event | category | flops | bytes accessed | tf_op | source)
XLA Modules:
  0.0 86.1 jit_solution(2015416441919567976)
XLA Ops:
  0.6 3.3 %collective-permute-start.1 = (bf16[256,1152]{1,0:T(8,128)(2,1)}, bf16[256,1152]{1,0:T(8,128)(2,1)S(1)}, u32[]{:S(2)}, u32[]{:S(2)}) collective-permute-start(bf16[256,1152]{1,0:T(8,128)(2,1)} %bitcast.15), channel_id=1, source_target_pairs={{0,2},{1,3},{2,0},{3,1},{4,6},{5,7},{6,4},{7,5},{8,10},{9,11},{10,... | collective-permute-start | bytes 1769480 | tf_op jit(solution)/shard_map/ppermute | solution.py:253
  4.0 0.1 collective-permute-start.3
  4.1 1.0 %collective-permute-start = (bf16[256,1152]{1,0:T(8,128)(2,1)}, bf16[256,1152]{1,0:T(8,128)(2,1)S(1)}, u32[]{:S(2)}, u32[]{:S(2)}) collective-permute-start(bf16[256,1152]{1,0:T(8,128)(2,1)} %bitcast.18), channel_id=1, source_target_pairs={{0,4},{1,5},{2,6},{3,7},{4,8},{5,9},{6,10},{7,11},{8,12},{9,13},{1... | collective-permute-start | bytes 1769480 | tf_op jit(solution)/shard_map/ppermute | solution.py:255
  6.4 0.1 pad_maximum_fusion.par_ref
  6.5 0.0 collective-permute-done.1.oimg
  6.5 1.0 %slice_select_fusion = bf16[128,1152]{1,0:T(8,128)(2,1)S(1)} fusion(bf16[256,1152]{1,0:T(8,128)(2,1)S(1)} %collective-permute-done.1.oimg, bf16[1,256,1152]{2,1,0:T(8,128)(2,1)} %param.6, pred[]{:T(512)S(6)} %eq.3), kind=kLoop, calls=%fused_computation | loop fusion | flops 147456 | bytes 884737 | tf_op jit(solution)/shard_map/jit(_where)/select_n | solution.py:257
  7.5 8.1 %collective-permute-start.2 = (bf16[128,1152]{1,0:T(8,128)(2,1)S(1)}, bf16[128,1152]{1,0:T(8,128)(2,1)S(1)}, u32[]{:S(2)}, u32[]{:S(2)}) collective-permute-start(bf16[128,1152]{1,0:T(8,128)(2,1)S(1)} %slice_select_fusion), channel_id=1, source_target_pairs={{0,248},{1,249},{2,250},{3,251},{4,252},{5,253},{6,254},{7,255},{8... | collective-permute-start | bytes 884744 | tf_op jit(solution)/shard_map/ppermute | solution.py:257
  15.6 1.1 %copy-done = bf16[1,256,1152]{2,1,0:T(8,128)(2,1)S(1)} copy-done((bf16[1,256,1152]{2,1,0:T(8,128)(2,1)S(1)}, bf16[1,256,1152]{2,1,0:T(8,128)(2,1)}, u32[]{:S(2)}) %copy-start) | copy-done | bytes 589848
  16.7 1.1 %copy-done.3 = bf16[1,256,1152]{2,1,0:T(8,128)(2,1)S(1)} copy-done((bf16[1,256,1152]{2,1,0:T(8,128)(2,1)S(1)}, bf16[1,256,1152]{2,1,0:T(8,128)(2,1)}, u32[]{:S(2)}) %copy-start.3) | copy-done | bytes 589848
  17.7 9.1 %shard_map.77 = (bf16[512,1152]{1,0:T(8,128)(2,1)S(1)}, bf16[512,1152]{1,0:T(8,128)(2,1)S(1)}, f32[512,1]{1,0:T(8,128)S(1)}, bf16[576,512]{1,0:T(8,128)(2,1)S(1)...) custom-call(s32[1]{0:T(128)} %bitcast.core_ref, ...), custom_call_target="tpu_custom_call" | custom-call | flops 4080000000 | bytes 8388608 | tf_op jit(solution)/shard_map/pallas_call | solution.py:262
  26.8 0.0 collective-permute-done.2.far
  26.8 0.0 copy-start.1
  26.9 1.1 %collective-permute-start.4 = (bf16[256,1152]{1,0:T(8,128)(2,1)S(1)}, bf16[256,1152]{1,0:T(8,128)(2,1)S(1)}, u32[]{:S(2)}, u32[]{:S(2)}) collective-permute-start(bf16[256,1152]{1,0:T(8,128)(2,1)S(1)} %collective-permute-done.near), channel_id=1, source_target_pairs={{0,2},{1,3},{2,0},{3,1},{4,6},{5,7},{6,4},{7,5},{8,10},{9,11},{10,... | collective-permute-start | bytes 1769480 | tf_op jit(solution)/shard_map/ppermute | solution.py:253
  27.9 0.3 collective-permute-start.5
  28.2 2.6 %shard_map.78 = (f32[256,1]{1,0:T(8,128)S(1)}, f32[512,1152]{1,0:T(8,128)S(1)}, f32[256,1152]{1,0:T(8,128)S(1)}, bf16[256,1152]{1,0:T(8,128)(2,1)S(1)}) custom-call(s32[1]{0:T(128)} %bitcast.core_ref, f32[2]{0:T(128)S(1)} %pad_maximum_fusion.par_ref, bf16[512,1152]{1,0:T(8,128)(2,1)S(1)} %get-tuple-element.42.zi, ...), custom_call_target="tpu_custom_call" | custom-call | flops 1360000000 | bytes 8388608 | tf_op jit(solution)/shard_map/pallas_call | solution.py:273
  30.8 0.0 collective-permute-done.4.near_o
  30.9 11.5 %shard_map.79 = (bf16[1152,1152]{1,0:T(8,128)(2,1)S(1)}, f32[1,256]{1,0:T(1,128)S(1)}, f32[1,256]{1,0:T(1,128)S(1)}) custom-call(s32[1]{0:T(128)} %bitcast.core_ref, f32[2]{0:T(128)S(1)} %pad_maximum_fusion.par_ref, bf16[256,1152]{1,0:T(8,128)(2,1)S(1)} %collective-permute-done.near, bf16[256,1152]{1,0:T(8,128)(2,1)S(1)} %collective-permute-done.4.near_o, ...), custom_call_target="tpu_custom_call" | custom-call | flops 6800000000 | bytes 8388608 | tf_op jit(solution)/shard_map/pallas_call | solution.py:278
  42.4 22.8 %all_to_all.22 = bf16[8,144,1152]{2,1,0:T(8,128)(2,1)S(1)} all-to-all(bf16[8,144,1152]{2,1,0:T(8,128)(2,1)S(1)} %bitcast.13), channel_id=1, replica_groups={{0,1,4,5,32,33,36,37},{2,10,18,26,226,234,242,250},{3,11,19,27,227,235,..., dimensions={0} | all-to-all | bytes 5308416 | tf_op jit(solution)/shard_map/all_to_all | solution.py:288
  65.2 1.5 %shard_map.80 = bf16[1408,128]{1,0:T(8,128)(2,1)} custom-call(bf16[1152,1152]{1,0:T(8,128)(2,1)S(1)} %bitcast.12), custom_call_target="tpu_custom_call" | custom-call | flops 10000000 | bytes 8388608 | tf_op jit(solution)/shard_map/pallas_call | solution.py:289
  66.6 5.3 %all-to-all-start.1 = ((bf16[16,88,128]{2,1,0:T(8,128)(2,1)}), bf16[16,88,128]{2,1,0:T(8,128)(2,1)S(1)}, u32[]{:S(2)}, u32[]{:S(2)}) async-start(bf16[16,88,128]{2,1,0:T(8,128)(2,1)} %bitcast.8), calls=%async_computation.1 | async-start | bytes 720896 | tf_op jit(solution)/shard_map/all_to_all | solution.py:292
  72.0 0.4 collective-permute-start.6
  72.3 5.6 %collective-permute-done.6.loss_far = f32[1,256]{1,0:T(1,128)S(1)} collective-permute-done((f32[1,256]{1,0:T(1,128)S(1)}, f32[1,256]{1,0:T(1,128)S(1)}, u32[]{:S(2)}, u32[]{:S(2)}) %collective-permute-start.6) | collective-permute-done | bytes 1056 | tf_op jit(solution)/shard_map/ppermute | solution.py:287
  77.9 7.5 %all-to-all-done.1 = bf16[16,88,128]{2,1,0:T(8,128)(2,1)S(1)} async-done(((bf16[16,88,128]{2,1,0:T(8,128)(2,1)}), bf16[16,88,128]{2,1,0:T(8,128)(2,1)S(1)}, u32[]{:S(2)}, u32[]{:S(2)}) %all-to-all-start.1) | async-done | bytes 360480 | tf_op jit(solution)/shard_map/all_to_all | solution.py:292
  85.4 0.7 shard_map.81
  (8 shorter events, 0.0 us)
Async XLA Ops:
  0.6 5.9 %collective-permute-start.1 = (bf16[256,1152]{1,0:T(8,128)(2,1)}, bf16[256,1152]{1,0:T(8,128)(2,1)S(1)}, u32[]{:S(2)}, u32[]{:S(2)}) collective-permute-start(bf16[256,1152]{1,0:T(8,128)(2,1)} %bitcast.15), channel_id=1, source_target_pairs={{0,2},{1,3},{2,0},{3,1},{4,6},{5,7},{6,4},{7,5},{8,10},{9,11},{10,... | collective-permute-start | bytes 1769480 | tf_op jit(solution)/shard_map/ppermute | solution.py:253
  4.0 11.6 %collective-permute-start.3 = (bf16[256,1152]{1,0:T(8,128)(2,1)}, bf16[256,1152]{1,0:T(8,128)(2,1)S(1)}, u32[]{:S(2)}, u32[]{:S(2)}) collective-permute-start(bf16[256,1152]{1,0:T(8,128)(2,1)} %bitcast.17), channel_id=1, source_target_pairs={{0,2},{1,3},{2,0},{3,1},{4,6},{5,7},{6,4},{7,5},{8,10},{9,11},{10,... | collective-permute-start | bytes 1769480 | tf_op jit(solution)/shard_map/ppermute | solution.py:253
  4.1 22.8 %collective-permute-start = (bf16[256,1152]{1,0:T(8,128)(2,1)}, bf16[256,1152]{1,0:T(8,128)(2,1)S(1)}, u32[]{:S(2)}, u32[]{:S(2)}) collective-permute-start(bf16[256,1152]{1,0:T(8,128)(2,1)} %bitcast.18), channel_id=1, source_target_pairs={{0,4},{1,5},{2,6},{3,7},{4,8},{5,9},{6,10},{7,11},{8,12},{9,13},{1... | collective-permute-start | bytes 1769480 | tf_op jit(solution)/shard_map/ppermute | solution.py:255
  7.5 19.3 %collective-permute-start.2 = (bf16[128,1152]{1,0:T(8,128)(2,1)S(1)}, bf16[128,1152]{1,0:T(8,128)(2,1)S(1)}, u32[]{:S(2)}, u32[]{:S(2)}) collective-permute-start(bf16[128,1152]{1,0:T(8,128)(2,1)S(1)} %slice_select_fusion), channel_id=1, source_target_pairs={{0,248},{1,249},{2,250},{3,251},{4,252},{5,253},{6,254},{7,255},{8... | collective-permute-start | bytes 884744 | tf_op jit(solution)/shard_map/ppermute | solution.py:257
  15.6 1.1 %copy-start = (bf16[1,256,1152]{2,1,0:T(8,128)(2,1)S(1)}, bf16[1,256,1152]{2,1,0:T(8,128)(2,1)}, u32[]{:S(2)}) copy-start(bf16[1,256,1152]{2,1,0:T(8,128)(2,1)} %param.6) | copy-start | bytes 1769476
  16.7 1.1 %copy-start.3 = (bf16[1,256,1152]{2,1,0:T(8,128)(2,1)S(1)}, bf16[1,256,1152]{2,1,0:T(8,128)(2,1)}, u32[]{:S(2)}) copy-start(bf16[1,256,1152]{2,1,0:T(8,128)(2,1)} %param.7) | copy-start | bytes 1769476
  17.7 13.1 %copy-start.2 = (bf16[1152,1152]{1,0:T(8,128)(2,1)S(1)}, bf16[1152,1152]{1,0:T(8,128)(2,1)}, u32[]{:S(2)}) copy-start(bf16[1152,1152]{1,0:T(8,128)(2,1)} %htxt.1) | copy-start | bytes 7962628
  26.8 4.0 %copy-start.1 = (bf16[1152,1152]{1,0:T(8,128)(2,1)S(1)}, bf16[1152,1152]{1,0:T(8,128)(2,1)}, u32[]{:S(2)}) copy-start(bf16[1152,1152]{1,0:T(8,128)(2,1)} %himg.1) | copy-start | bytes 7962628
  26.9 4.0 %collective-permute-start.4 = (bf16[256,1152]{1,0:T(8,128)(2,1)S(1)}, bf16[256,1152]{1,0:T(8,128)(2,1)S(1)}, u32[]{:S(2)}, u32[]{:S(2)}) collective-permute-start(bf16[256,1152]{1,0:T(8,128)(2,1)S(1)} %collective-permute-done.near), channel_id=1, source_target_pairs={{0,2},{1,3},{2,0},{3,1},{4,6},{5,7},{6,4},{7,5},{8,10},{9,11},{10,... | collective-permute-start | bytes 1769480 | tf_op jit(solution)/shard_map/ppermute | solution.py:253
  27.9 2.9 %collective-permute-start.5 = (bf16[128,1152]{1,0:T(8,128)(2,1)S(1)}, bf16[128,1152]{1,0:T(8,128)(2,1)S(1)}, u32[]{:S(2)}, u32[]{:S(2)}) collective-permute-start(bf16[128,1152]{1,0:T(8,128)(2,1)S(1)} %collective-permute-done.2.far), channel_id=1, source_target_pairs={{0,2},{1,3},{2,0},{3,1},{4,6},{5,7},{6,4},{7,5},{8,10},{9,11},{10,... | collective-permute-start | bytes 884744 | tf_op jit(solution)/shard_map/ppermute | solution.py:253
  66.6 18.8 %all-to-all-start.1 = ((bf16[16,88,128]{2,1,0:T(8,128)(2,1)}), bf16[16,88,128]{2,1,0:T(8,128)(2,1)S(1)}, u32[]{:S(2)}, u32[]{:S(2)}) async-start(bf16[16,88,128]{2,1,0:T(8,128)(2,1)} %bitcast.8), calls=%async_computation.1 | async-start | bytes 720896 | tf_op jit(solution)/shard_map/all_to_all | solution.py:292
  72.0 5.9 %collective-permute-start.6 = (f32[1,256]{1,0:T(1,128)S(1)}, f32[1,256]{1,0:T(1,128)S(1)}, u32[]{:S(2)}, u32[]{:S(2)}) collective-permute-start(f32[1,256]{1,0:T(1,128)S(1)} %get-tuple-element.57), channel_id=1, source_target_pairs={{0,8},{1,9},{2,10},{3,11},{4,12},{5,13},{6,14},{7,15},{8,16},{9,17... | collective-permute-start | bytes 3080 | tf_op jit(solution)/shard_map/ppermute | solution.py:287

commit v6 on v5

--- a/solution.py
+++ b/solution.py
@@ -175,19 +175,19 @@
     zf, inv_t = normalise(ft[...], htxt[...])
     zft[...] = zf
     zt[...] = zf.astype(BF16)
+    score(z2[...], zown[HI], scale, bias, None, gt2, kept2)
+    score(zi[...], zt[...], scale, bias, None, gts, kept)
     ft2[...] = dot(pick[...], f2[...], NT).astype(BF16)
     ftt[...] = dot(pick[...], ft[...], NT).astype(BF16)
-    score(z2[...], zown[HI], scale, bias, None, gt2, kept2)
-    score(zi[...], zt[...], scale, bias, None, gts, kept)
-    loss = loss_near[...] + softplus_rows(kept[pl.ds(pl.multiple_of(c * BLOCK, BLOCK), BLOCK)])
-    loss_out[...] = jnp.transpose(jnp.broadcast_to(loss, (BLOCK, 128)))[:1]
-    loss_far[...] = jnp.transpose(jnp.broadcast_to(softplus_rows(kept2[...]), (BLOCK, 128)))[:1]
     du_i[end] = backnorm(dot(gt2[...], zown[HI]), zf2[...], inv2)
     du_t[2 * BLOCK : 3 * BLOCK] = du3[...]
     du_t[3 * BLOCK :] = backnorm(g4[...] + dot(gt2[...], z2[...], TN), zown[HI].astype(F32) + lzown[HI], invown[HI])
     pair = slice(0, 2 * BLOCK)
     du_i[pair] = backnorm(dq[...] + dot(gts[...], zt[...]), zi[...].astype(F32) + lzi[...], inv[...])
     du_t[pair] = backnorm(dot(gts[...], zi[...], TN), zft[...], inv_t)
+    loss = loss_near[...] + softplus_rows(kept[pl.ds(pl.multiple_of(c * BLOCK, BLOCK), BLOCK)])
+    loss_out[...] = jnp.transpose(jnp.broadcast_to(loss, (BLOCK, 128)))[:1]
+    loss_far[...] = jnp.transpose(jnp.broadcast_to(softplus_rows(kept2[...]), (BLOCK, 128)))[:1]
     for first in range(0, WIDTH, 256):
         cols = slice(first, min(first + 256, WIDTH))
         g_i = dot(fti[...], du_i[: 2 * BLOCK, cols]) + dot(ft2[...], du_i[end, cols])

time: 86.5 us -> 86.6 us (level)
  no operation moved by 1% of the time
where the time goes in v6:
time: 86.6 us; the launch traced here: 86.3 us
  Pallas kernels  25.6 us (30%)
  blocking collectives  22.8 us (26%)
  starting transfers between devices  19.6 us (23%)
  waiting for transfers between devices  13.1 us (15%)
  local copies, waits for them, and re-layouts  2.14 us (2%)
  between operations  2.07 us (2%)
  other arithmetic  1.07 us (1%)
    all_to_all x1, blocking collectives, local(): lax.all_to_all(term, AXES, 0, 0, axis_index_groups=first_groups(), tiled=...  22.8 us
    pallas_call x1, Pallas kernels, local(): call(late_kernel, shapes(BF16, square) + shapes(F32, (1, BLOCK), (1, BLOC...  11.7 us
    pallas_call x1, Pallas kernels, local(): call(early_kernel, shapes(BF16, two, two) + shapes(F32, (512, 1)) + shape...  9.08 us
    ppermute x1, starting transfers between devices, local(): lax.ppermute(jnp.where(first, img[:128], other_img[128:]), AXES, chip_shi...  8.1 us
    all_to_all x1, waiting for transfers between devices, local(): lax.all_to_all(half, AXES, 0, 0, axis_index_groups=second_groups(), tiled...  7.49 us
    ppermute x1, waiting for transfers between devices, local(): loss_far = lax.ppermute(loss_far, AXES, chip_shift(2))  5.56 us
    all_to_all x1, starting transfers between devices, local(): lax.all_to_all(half, AXES, 0, 0, axis_index_groups=second_groups(), tiled...  5.35 us
    ppermute x4, starting transfers between devices, swap(): return lax.ppermute(a, AXES, core_swap())  4.77 us
  transfers between devices with their start and end apart: 8, of which 2 were waited for; matrix products, arithmetic and copies ran while one was open for 1% of the time, Pallas kernels for 14%

profile of v6, /device:TPU:1, one launch (start us, length us, event | category | flops | bytes accessed | tf_op | source)
XLA Modules:
  0.0 86.3 jit_solution(13591611874150956290)
XLA Ops:
  0.6 3.3 %collective-permute-start.1 = (bf16[256,1152]{1,0:T(8,128)(2,1)}, bf16[256,1152]{1,0:T(8,128)(2,1)S(1)}, u32[]{:S(2)}, u32[]{:S(2)}) collective-permute-start(bf16[256,1152]{1,0:T(8,128)(2,1)} %bitcast.15), channel_id=1, source_target_pairs={{0,2},{1,3},{2,0},{3,1},{4,6},{5,7},{6,4},{7,5},{8,10},{9,11},{10,... | collective-permute-start | bytes 1769480 | tf_op jit(solution)/shard_map/ppermute | solution.py:253
  4.0 0.1 collective-permute-start.3
  4.1 1.0 %collective-permute-start = (bf16[256,1152]{1,0:T(8,128)(2,1)}, bf16[256,1152]{1,0:T(8,128)(2,1)S(1)}, u32[]{:S(2)}, u32[]{:S(2)}) collective-permute-start(bf16[256,1152]{1,0:T(8,128)(2,1)} %bitcast.18), channel_id=1, source_target_pairs={{0,4},{1,5},{2,6},{3,7},{4,8},{5,9},{6,10},{7,11},{8,12},{9,13},{1... | collective-permute-start | bytes 1769480 | tf_op jit(solution)/shard_map/ppermute | solution.py:255
  6.4 0.1 pad_maximum_fusion.par_ref
  6.5 0.0 collective-permute-done.1.oimg
  6.5 1.0 %slice_select_fusion = bf16[128,1152]{1,0:T(8,128)(2,1)S(1)} fusion(bf16[256,1152]{1,0:T(8,128)(2,1)S(1)} %collective-permute-done.1.oimg, bf16[1,256,1152]{2,1,0:T(8,128)(2,1)} %param.6, pred[]{:T(512)S(6)} %eq.3), kind=kLoop, calls=%fused_computation | loop fusion | flops 147456 | bytes 884737 | tf_op jit(solution)/shard_map/jit(_where)/select_n | solution.py:257
  7.5 8.1 %collective-permute-start.2 = (bf16[128,1152]{1,0:T(8,128)(2,1)S(1)}, bf16[128,1152]{1,0:T(8,128)(2,1)S(1)}, u32[]{:S(2)}, u32[]{:S(2)}) collective-permute-start(bf16[128,1152]{1,0:T(8,128)(2,1)S(1)} %slice_select_fusion), channel_id=1, source_target_pairs={{0,248},{1,249},{2,250},{3,251},{4,252},{5,253},{6,254},{7,255},{8... | collective-permute-start | bytes 884744 | tf_op jit(solution)/shard_map/ppermute | solution.py:257
  15.6 0.0 collective-permute-done.3.otxt
  15.6 1.1 %copy-done = bf16[1,256,1152]{2,1,0:T(8,128)(2,1)S(1)} copy-done((bf16[1,256,1152]{2,1,0:T(8,128)(2,1)S(1)}, bf16[1,256,1152]{2,1,0:T(8,128)(2,1)}, u32[]{:S(2)}) %copy-start) | copy-done | bytes 589848
  16.7 1.1 %copy-done.3 = bf16[1,256,1152]{2,1,0:T(8,128)(2,1)S(1)} copy-done((bf16[1,256,1152]{2,1,0:T(8,128)(2,1)S(1)}, bf16[1,256,1152]{2,1,0:T(8,128)(2,1)}, u32[]{:S(2)}) %copy-start.3) | copy-done | bytes 589848
  17.7 9.1 %shard_map.77 = (bf16[512,1152]{1,0:T(8,128)(2,1)S(1)}, bf16[512,1152]{1,0:T(8,128)(2,1)S(1)}, f32[512,1]{1,0:T(8,128)S(1)}, bf16[576,512]{1,0:T(8,128)(2,1)S(1)...) custom-call(s32[1]{0:T(128)} %bitcast.core_ref, ...), custom_call_target="tpu_custom_call" | custom-call | flops 4080000000 | bytes 8388608 | tf_op jit(solution)/shard_map/pallas_call | solution.py:262
  26.8 0.0 collective-permute-done.near
  26.8 0.0 copy-start.1
  26.9 1.1 %collective-permute-start.4 = (bf16[256,1152]{1,0:T(8,128)(2,1)S(1)}, bf16[256,1152]{1,0:T(8,128)(2,1)S(1)}, u32[]{:S(2)}, u32[]{:S(2)}) collective-permute-start(bf16[256,1152]{1,0:T(8,128)(2,1)S(1)} %collective-permute-done.near), channel_id=1, source_target_pairs={{0,2},{1,3},{2,0},{3,1},{4,6},{5,7},{6,4},{7,5},{8,10},{9,11},{10,... | collective-permute-start | bytes 1769480 | tf_op jit(solution)/shard_map/ppermute | solution.py:253
  27.9 0.3 collective-permute-start.5
  28.2 2.6 %shard_map.78 = (f32[256,1]{1,0:T(8,128)S(1)}, f32[512,1152]{1,0:T(8,128)S(1)}, f32[256,1152]{1,0:T(8,128)S(1)}, bf16[256,1152]{1,0:T(8,128)(2,1)S(1)}) custom-call(s32[1]{0:T(128)} %bitcast.core_ref, f32[2]{0:T(128)S(1)} %pad_maximum_fusion.par_ref, bf16[512,1152]{1,0:T(8,128)(2,1)S(1)} %get-tuple-element.42.zi, ...), custom_call_target="tpu_custom_call" | custom-call | flops 1360000000 | bytes 8388608 | tf_op jit(solution)/shard_map/pallas_call | solution.py:273
  30.9 11.7 %shard_map.79 = (bf16[1152,1152]{1,0:T(8,128)(2,1)S(1)}, f32[1,256]{1,0:T(1,128)S(1)}, f32[1,256]{1,0:T(1,128)S(1)}) custom-call(s32[1]{0:T(128)} %bitcast.core_ref, f32[2]{0:T(128)S(1)} %pad_maximum_fusion.par_ref, bf16[256,1152]{1,0:T(8,128)(2,1)S(1)} %collective-permute-done.near, bf16[256,1152]{1,0:T(8,128)(2,1)S(1)} %collective-permute-done.4.near_o, ...), custom_call_target="tpu_custom_call" | custom-call | flops 6800000000 | bytes 8388608 | tf_op jit(solution)/shard_map/pallas_call | solution.py:278
  42.5 22.8 %all_to_all.22 = bf16[8,144,1152]{2,1,0:T(8,128)(2,1)S(1)} all-to-all(bf16[8,144,1152]{2,1,0:T(8,128)(2,1)S(1)} %bitcast.13), channel_id=1, replica_groups={{0,1,4,5,32,33,36,37},{2,10,18,26,226,234,242,250},{3,11,19,27,227,235,..., dimensions={0} | all-to-all | bytes 5308416 | tf_op jit(solution)/shard_map/all_to_all | solution.py:288
  65.3 1.5 %shard_map.80 = bf16[1408,128]{1,0:T(8,128)(2,1)} custom-call(bf16[1152,1152]{1,0:T(8,128)(2,1)S(1)} %bitcast.12), custom_call_target="tpu_custom_call" | custom-call | flops 10000000 | bytes 8388608 | tf_op jit(solution)/shard_map/pallas_call | solution.py:289
  66.8 5.3 %all-to-all-start.1 = ((bf16[16,88,128]{2,1,0:T(8,128)(2,1)}), bf16[16,88,128]{2,1,0:T(8,128)(2,1)S(1)}, u32[]{:S(2)}, u32[]{:S(2)}) async-start(bf16[16,88,128]{2,1,0:T(8,128)(2,1)} %bitcast.8), calls=%async_computation.1 | async-start | bytes 720896 | tf_op jit(solution)/shard_map/all_to_all | solution.py:292
  72.2 0.4 collective-permute-start.6
  72.5 5.6 %collective-permute-done.6.loss_far = f32[1,256]{1,0:T(1,128)S(1)} collective-permute-done((f32[1,256]{1,0:T(1,128)S(1)}, f32[1,256]{1,0:T(1,128)S(1)}, u32[]{:S(2)}, u32[]{:S(2)}) %collective-permute-start.6) | collective-permute-done | bytes 1056 | tf_op jit(solution)/shard_map/ppermute | solution.py:287
  78.1 7.5 %all-to-all-done.1 = bf16[16,88,128]{2,1,0:T(8,128)(2,1)S(1)} async-done(((bf16[16,88,128]{2,1,0:T(8,128)(2,1)}), bf16[16,88,128]{2,1,0:T(8,128)(2,1)S(1)}, u32[]{:S(2)}, u32[]{:S(2)}) %all-to-all-start.1) | async-done | bytes 360480 | tf_op jit(solution)/shard_map/all_to_all | solution.py:292
  85.6 0.7 shard_map.81
  (8 shorter events, 0.0 us)
Async XLA Ops:
  0.6 5.9 %collective-permute-start.1 = (bf16[256,1152]{1,0:T(8,128)(2,1)}, bf16[256,1152]{1,0:T(8,128)(2,1)S(1)}, u32[]{:S(2)}, u32[]{:S(2)}) collective-permute-start(bf16[256,1152]{1,0:T(8,128)(2,1)} %bitcast.15), channel_id=1, source_target_pairs={{0,2},{1,3},{2,0},{3,1},{4,6},{5,7},{6,4},{7,5},{8,10},{9,11},{10,... | collective-permute-start | bytes 1769480 | tf_op jit(solution)/shard_map/ppermute | solution.py:253
  4.0 11.6 %collective-permute-start.3 = (bf16[256,1152]{1,0:T(8,128)(2,1)}, bf16[256,1152]{1,0:T(8,128)(2,1)S(1)}, u32[]{:S(2)}, u32[]{:S(2)}) collective-permute-start(bf16[256,1152]{1,0:T(8,128)(2,1)} %bitcast.17), channel_id=1, source_target_pairs={{0,2},{1,3},{2,0},{3,1},{4,6},{5,7},{6,4},{7,5},{8,10},{9,11},{10,... | collective-permute-start | bytes 1769480 | tf_op jit(solution)/shard_map/ppermute | solution.py:253
  4.1 22.8 %collective-permute-start = (bf16[256,1152]{1,0:T(8,128)(2,1)}, bf16[256,1152]{1,0:T(8,128)(2,1)S(1)}, u32[]{:S(2)}, u32[]{:S(2)}) collective-permute-start(bf16[256,1152]{1,0:T(8,128)(2,1)} %bitcast.18), channel_id=1, source_target_pairs={{0,4},{1,5},{2,6},{3,7},{4,8},{5,9},{6,10},{7,11},{8,12},{9,13},{1... | collective-permute-start | bytes 1769480 | tf_op jit(solution)/shard_map/ppermute | solution.py:255
  7.5 19.3 %collective-permute-start.2 = (bf16[128,1152]{1,0:T(8,128)(2,1)S(1)}, bf16[128,1152]{1,0:T(8,128)(2,1)S(1)}, u32[]{:S(2)}, u32[]{:S(2)}) collective-permute-start(bf16[128,1152]{1,0:T(8,128)(2,1)S(1)} %slice_select_fusion), channel_id=1, source_target_pairs={{0,248},{1,249},{2,250},{3,251},{4,252},{5,253},{6,254},{7,255},{8... | collective-permute-start | bytes 884744 | tf_op jit(solution)/shard_map/ppermute | solution.py:257
  15.6 1.1 %copy-start = (bf16[1,256,1152]{2,1,0:T(8,128)(2,1)S(1)}, bf16[1,256,1152]{2,1,0:T(8,128)(2,1)}, u32[]{:S(2)}) copy-start(bf16[1,256,1152]{2,1,0:T(8,128)(2,1)} %param.6) | copy-start | bytes 1769476
  16.7 1.1 %copy-start.3 = (bf16[1,256,1152]{2,1,0:T(8,128)(2,1)S(1)}, bf16[1,256,1152]{2,1,0:T(8,128)(2,1)}, u32[]{:S(2)}) copy-start(bf16[1,256,1152]{2,1,0:T(8,128)(2,1)} %param.7) | copy-start | bytes 1769476
  17.7 13.1 %copy-start.2 = (bf16[1152,1152]{1,0:T(8,128)(2,1)S(1)}, bf16[1152,1152]{1,0:T(8,128)(2,1)}, u32[]{:S(2)}) copy-start(bf16[1152,1152]{1,0:T(8,128)(2,1)} %htxt.1) | copy-start | bytes 7962628
  26.8 4.0 %copy-start.1 = (bf16[1152,1152]{1,0:T(8,128)(2,1)S(1)}, bf16[1152,1152]{1,0:T(8,128)(2,1)}, u32[]{:S(2)}) copy-start(bf16[1152,1152]{1,0:T(8,128)(2,1)} %himg.1) | copy-start | bytes 7962628
  26.9 4.0 %collective-permute-start.4 = (bf16[256,1152]{1,0:T(8,128)(2,1)S(1)}, bf16[256,1152]{1,0:T(8,128)(2,1)S(1)}, u32[]{:S(2)}, u32[]{:S(2)}) collective-permute-start(bf16[256,1152]{1,0:T(8,128)(2,1)S(1)} %collective-permute-done.near), channel_id=1, source_target_pairs={{0,2},{1,3},{2,0},{3,1},{4,6},{5,7},{6,4},{7,5},{8,10},{9,11},{10,... | collective-permute-start | bytes 1769480 | tf_op jit(solution)/shard_map/ppermute | solution.py:253
  27.9 2.9 %collective-permute-start.5 = (bf16[128,1152]{1,0:T(8,128)(2,1)S(1)}, bf16[128,1152]{1,0:T(8,128)(2,1)S(1)}, u32[]{:S(2)}, u32[]{:S(2)}) collective-permute-start(bf16[128,1152]{1,0:T(8,128)(2,1)S(1)} %collective-permute-done.2.far), channel_id=1, source_target_pairs={{0,2},{1,3},{2,0},{3,1},{4,6},{5,7},{6,4},{7,5},{8,10},{9,11},{10,... | collective-permute-start | bytes 884744 | tf_op jit(solution)/shard_map/ppermute | solution.py:253
  66.8 18.8 %all-to-all-start.1 = ((bf16[16,88,128]{2,1,0:T(8,128)(2,1)}), bf16[16,88,128]{2,1,0:T(8,128)(2,1)S(1)}, u32[]{:S(2)}, u32[]{:S(2)}) async-start(bf16[16,88,128]{2,1,0:T(8,128)(2,1)} %bitcast.8), calls=%async_computation.1 | async-start | bytes 720896 | tf_op jit(solution)/shard_map/all_to_all | solution.py:292
  72.2 5.9 %collective-permute-start.6 = (f32[1,256]{1,0:T(1,128)S(1)}, f32[1,256]{1,0:T(1,128)S(1)}, u32[]{:S(2)}, u32[]{:S(2)}) collective-permute-start(f32[1,256]{1,0:T(1,128)S(1)} %get-tuple-element.57), channel_id=1, source_target_pairs={{0,8},{1,9},{2,10},{3,11},{4,12},{5,13},{6,14},{7,15},{8,16},{9,17... | collective-permute-start | bytes 3080 | tf_op jit(solution)/shard_map/ppermute | solution.py:287
